TPU v7x, 128 devices: a whole 4x4x4 slice. The times are simulated.
128 devices in a mesh: arc: 8 (over y, x_hi), trow: 4 (over z), tcol: 4 (over x_lo, core).
Axes of the slice: x: 4 (x_hi: 2, x_lo: 2; x = x_hi * 2 + x_lo), y: 4, z: 4, core: 2. Of those that a mesh axis runs over, the one named last changes fastest.
Arguments:
- design: bfloat16 [5120, 8192], P('arc', 'tcol'), may hold values from -0.125 to 0.125
- local_design: bfloat16 [5120, 128], P('arc'), may hold values from -0.3125 to 0.3125
- lengths: int32 [16], P('arc'), may hold values from 1 to 320, 3840 in all
- regularizer: float32 [8192], P(('arc', 'trow')), may hold values from 0.2 to 2
Outputs:
- normal: float32 [8192, 8192], P(('arc', 'trow'), 'tcol')
- panel_factor: float32 [2, 8192, 512], P(None, 'tcol')
Inputs may be any that keep to these rules, and one draw needn't show every extreme that they name: `lengths`: each arc has at least one live row; some arc is full.
All inputs are finite; a program needn't handle non-finite values. No bound on the sum of `lengths` on one device may be relied on, other than what follows from the above.
Results may differ from a plain program's by a relative error of at most 0.003.
Values may be sent and summed in bfloat16 or wider, within the bound.
A program may use at most 128 MiB of HBM per device.

v0:
```python
import jax
import jax.numpy as jnp
from jax import lax
from jax.sharding import PartitionSpec as P

PANEL = 512
PANELS = 2


ridge = 0.1


def broadcast(block, axis, holder):
    block = jnp.where(lax.axis_index(axis) == holder, block, jnp.zeros_like(block))
    return lax.psum(block, axis)


def project_arcs(design, local_design, lengths):
    arc_count = lengths.shape[0]
    row_count = design.shape[0]
    capacity = row_count // arc_count
    arc_blocks = design.reshape(arc_count, capacity, design.shape[1])
    local_half = local_design.reshape(arc_count, capacity, local_design.shape[1])
    live_rows = jnp.arange(capacity, dtype=jnp.int32)[None, :] < lengths[:, None]
    arc_blocks = jnp.where(live_rows[:, :, None], arc_blocks, jnp.zeros((), design.dtype))
    local_half = jnp.where(live_rows[:, :, None], local_half, jnp.zeros((), local_design.dtype))
    local_normal = jnp.einsum(
        "acl,acm->alm", local_half, local_half, preferred_element_type=jnp.float32
    )
    local_normal = local_normal + ridge * jnp.eye(local_half.shape[2], dtype=jnp.float32)[None]
    local_factor = jnp.linalg.cholesky(local_normal)
    local_cols = local_half.astype(jnp.float32)
    basis_rows = lax.linalg.triangular_solve(
        local_factor, jnp.transpose(local_cols, (0, 2, 1)), left_side=True, lower=True
    )
    basis_rows = basis_rows.astype(jnp.bfloat16)
    loadings = jnp.einsum(
        "alc,acw->alw", basis_rows, arc_blocks, preferred_element_type=jnp.float32
    ).astype(jnp.bfloat16)
    cleaned = arc_blocks.astype(jnp.float32) - jnp.einsum(
        "alc,alw->acw", basis_rows, loadings, preferred_element_type=jnp.float32
    )
    return cleaned.astype(jnp.bfloat16).reshape(row_count, design.shape[1])


def contract_rows(left_rows, right_rows):
    return lax.dot_general(
        left_rows, right_rows, (((0,), (0,)), ((), ())), preferred_element_type=jnp.float32
    )


def per_device(design, local_design, lengths, regularizer):
    row_count, col_width = design.shape
    tile_rows = regularizer.shape[0]
    arc_total = lax.axis_size("arc")
    trow_total = lax.axis_size("trow")
    trow_index = lax.axis_index("trow")
    row_start = (lax.axis_index("arc") * trow_total + trow_index) * tile_rows
    col_start = lax.axis_index("tcol") * col_width
    projected = project_arcs(design, local_design, lengths)
    gathered = lax.all_gather(projected, "tcol", axis=1, tiled=True)
    regrouped = gathered.reshape(row_count, arc_total, trow_total, tile_rows)
    selected = lax.dynamic_slice_in_dim(regrouped, trow_index, 1, 2).reshape(
        row_count, arc_total * tile_rows
    )
    normal_block = lax.psum_scatter(
        contract_rows(selected, projected), "arc", scatter_dimension=0, tiled=True
    )
    rows_global = row_start + jnp.arange(tile_rows, dtype=jnp.int32)
    cols_global = col_start + jnp.arange(col_width, dtype=jnp.int32)
    on_diagonal = rows_global[:, None] == cols_global[None, :]
    normal_block = normal_block + jnp.where(
        on_diagonal, regularizer[:, None], jnp.zeros((), jnp.float32)
    )
    panel_factors = []
    for panel_index in range(PANELS):
        lead_col = panel_index * PANEL
        padded_rows = jnp.pad(normal_block, ((PANEL, PANEL), (0, 0)))
        slice_start = jnp.clip(lead_col - row_start + PANEL, 0, tile_rows + PANEL)
        slice_rows = lax.dynamic_slice_in_dim(padded_rows, slice_start, PANEL, 0)
        panel_global = lead_col + jnp.arange(PANEL, dtype=jnp.int32)
        in_tile = (panel_global >= row_start) & (panel_global < row_start + tile_rows)
        own_share = jnp.where(in_tile[:, None], slice_rows, jnp.zeros((), jnp.float32))
        panel_strip = lax.psum(own_share, ("arc", "trow"))
        pivot_block, row_strip = (
            broadcast(panel_strip[:, lead_col : lead_col + PANEL], "tcol", 0),
            broadcast(normal_block[:, lead_col : lead_col + PANEL], "tcol", 0),
        )
        lower_factor = jnp.linalg.cholesky(pivot_block)
        col_factor = lax.linalg.triangular_solve(
            lower_factor, panel_strip, left_side=True, lower=True
        ).T
        row_factor = lax.linalg.triangular_solve(
            lower_factor, row_strip.T, left_side=True, lower=True
        ).T
        col_factor = jnp.where(
            cols_global[:, None] >= lead_col, col_factor, jnp.zeros((), jnp.float32)
        )
        row_factor = jnp.where(
            rows_global[:, None] >= lead_col, row_factor, jnp.zeros((), jnp.float32)
        )
        normal_block = normal_block - jnp.dot(
            row_factor, col_factor.T, precision=lax.Precision.HIGHEST
        )
        panel_factors.append(col_factor)
    return (normal_block, jnp.stack(panel_factors))


def solution(mesh):
    return jax.shard_map(
        per_device,
        mesh=mesh,
        in_specs=(P("arc", "tcol"), P("arc", None), P("arc"), P(("arc", "trow"))),
        out_specs=(P(("arc", "trow"), "tcol"), P(None, "tcol", None)),
        check_vma=False,
    )
```

profile of v0, /device:TPU:0, one launch (start us, length us, event | category | flops | bytes accessed | tf_op | source)
XLA Modules:
  0.0 1568.0 jit_solution(3386765637183662593)
XLA Ops:
  9.6 23.5 %custom-call.33 = f32[2,128,128]{2,1,0:T(8,128)S(1)} custom-call(f32[2,128,128]{2,1,0:T(8,128)S(1)} %fusion.97), custom_call_target="Cholesky" | custom-call | tf_op jit(solution)/shard_map/jit(cholesky)/cholesky | solution.py:31
  33.4 19.7 %custom-call.34 = f32[2,1,128,128]{2,3,1,0:T(8,128)S(1)} custom-call(f32[2,1,128,128]{3,2,1,0:T(8,128)S(1)} %select_bitcast_fusion), custom_call_target="InvertDiagBlocksLowerTriangular" | custom-call | tf_op jit(solution)/shard_map/triangular_solve | solution.py:33
  61.2 99.7 %all-gather.2.cloned.1.call-done = bf16[640,8192]{0,1:T(8,128)(2,1)} async-done(((bf16[640,2048]{0,1:T(8,128)(2,1)}), bf16[640,8192]{0,1:T(8,128)(2,1)}) %all-gather.2.cloned.1.call-update) | async-done | bytes 10485776 | tf_op jit(solution)/shard_map/all_gather | solution.py:61
  162.9 10.2 fusion.158
  173.2 195.0 %reduce-scatter.2.cloned.1.call-done = f32[256,2048]{0,1:T(8,128)} async-done(((f32[2048,2048]{0,1:T(8,128)}), f32[256,2048]{0,1:T(8,128)}) %reduce-scatter.2.cloned.1.call-update) | async-done | bytes 2097168 | tf_op jit(solution)/shard_map/reduce_scatter | solution.py:66
  374.1 363.9 %all-reduce.10.cloned.1.call-done = f32[512,2048]{0,1:T(8,128)} async-done(((f32[512,2048]{0,1:T(8,128)}), f32[512,2048]{0,1:T(8,128)}) %all-reduce.10.cloned.1.call-update) | async-done | bytes 4194320 | tf_op jit(solution)/shard_map/psum | solution.py:84
  740.4 50.1 %all-reduce.16.cloned.1.call-done = (f32[512,512]{0,1:T(8,128)}, f32[512,256]{1,0:T(8,128)}) async-done(((f32[512,512]{0,1:T(8,128)}, f32[512,256]{1,0:T(8,128)}), (f32[512,512]{0,1:T(8,128)}, f32[512,256]{1,0:T(8,128)})) %all-reduce.16.cloned.1.call-update) | async-done | bytes 1572880 | tf_op jit(solution)/shard_map/psum | solution.py:15
  793.6 11.7 cholesky.327
  805.5 9.8 custom-call.40
  815.9 11.7 cholesky.346
  827.7 10.2 custom-call.41
  838.6 11.7 cholesky.367
  850.3 9.8 custom-call.42
  860.7 11.7 cholesky.384
  885.5 39.3 %custom-call.43 = f32[4,128,128]{1,2,0:T(8,128)S(1)} custom-call(f32[4,128,128]{2,1,0:T(8,128)S(1)} %get-tuple-element.33), custom_call_target="InvertDiagBlocksLowerTriangular" | custom-call | tf_op jit(solution)/shard_map/triangular_solve/custom-call.9 | solution.py:93
  964.8 364.2 %all-reduce.12.cloned.1.call-done = f32[512,2048]{0,1:T(8,128)} async-done(((f32[512,2048]{0,1:T(8,128)}), f32[512,2048]{0,1:T(8,128)}) %all-reduce.12.cloned.1.call-update) | async-done | bytes 4194320 | tf_op jit(solution)/shard_map/psum | solution.py:84
  1334.8 46.8 %all-reduce.14.cloned.1.call-done = (f32[512,512]{0,1:T(8,128)}, f32[512,256]{1,0:T(8,128)}) async-done(((f32[512,512]{0,1:T(8,128)}, f32[512,256]{1,0:T(8,128)}), (f32[512,512]{0,1:T(8,128)}, f32[512,256]{1,0:T(8,128)})) %all-reduce.14.cloned.1.call-update) | async-done | bytes 1572880 | tf_op jit(solution)/shard_map/psum | solution.py:15
  1384.6 11.7 cholesky.399
  1406.9 11.7 cholesky.418
  1418.7 10.2 custom-call.46
  1429.6 11.7 cholesky.439
  1441.3 9.8 custom-call.47
  1451.7 11.7 cholesky.456
  1476.5 39.3 %custom-call.48 = f32[4,128,128]{1,2,0:T(8,128)S(1)} custom-call(f32[4,128,128]{2,1,0:T(8,128)S(1)} %get-tuple-element.35), custom_call_target="InvertDiagBlocksLowerTriangular" | custom-call | tf_op jit(solution)/shard_map/triangular_solve/custom-call.9 | solution.py:93
  (192 shorter events, 168.0 us)
Async XLA Ops:
  7.2 153.7 %all-gather.2.cloned.1.call-start = ((), (), s32[]{:S(2)}) async-start(), calls=%async_computation.1 | async-start | bytes 13107200 | tf_op jit(solution)/shard_map/all_gather | solution.py:61
  61.0 307.3 %reduce-scatter.2.cloned.1.call-start = ((), (), s32[]{:S(2)}) async-start(), calls=%async_computation.2 | async-start | bytes 18874368 | tf_op jit(solution)/shard_map/reduce_scatter | solution.py:66
  173.0 195.2 %copy-start.18 = (f32[256]{0:T(256)S(1)}, f32[256]{0:T(256)}, u32[]{:S(2)}) copy-start(f32[256]{0:T(256)} %param.12) | copy-start | bytes 3076
  173.1 564.9 %all-reduce.10.cloned.1.call-start = ((), (), s32[]{:S(2)}) async-start(), calls=%async_computation.3 | async-start | bytes 8388608 | tf_op jit(solution)/shard_map/psum | solution.py:84
  370.0 3.3 copy-start
  373.2 417.4 %all-reduce.16.cloned.1.call-start = ((), (), s32[]{:S(2)}) async-start(), calls=%async_computation.6 | async-start | bytes 3145728 | tf_op jit(solution)/shard_map/psum | solution.py:15
  740.3 588.7 %all-reduce.12.cloned.1.call-start = ((), (), s32[]{:S(2)}) async-start(), calls=%async_computation.4 | async-start | bytes 8388608 | tf_op jit(solution)/shard_map/psum | solution.py:84
  885.5 48.4 %copy-start.3 = (f32[512,512]{1,0:T(8,128)}, f32[512,512]{1,0:T(8,128)S(1)}, u32[]{:S(2)}) copy-start(f32[512,512]{1,0:T(8,128)S(1)} %get-tuple-element.206) | copy-start | bytes 3145732
  941.0 8.3 copy-start.16
  941.1 13.2 copy-start.1
  941.1 13.2 copy-start.4
  941.1 13.2 copy-start.6
  941.1 13.2 copy-start.8
  949.3 8.9 copy-start.10
  962.7 368.6 %copy-start.5 = (f32[128,2048]{0,1:T(8,128)S(1)}, f32[128,2048]{0,1:T(8,128)}, u32[]{:S(2)}) copy-start(f32[128,2048]{0,1:T(8,128)} %copy.69) | copy-start | bytes 3145732
  962.7 368.6 %copy-start.7 = (f32[128,2048]{0,1:T(8,128)S(1)}, f32[128,2048]{0,1:T(8,128)}, u32[]{:S(2)}) copy-start(f32[128,2048]{0,1:T(8,128)} %copy.70) | copy-start | bytes 3145732
  962.7 368.6 %copy-start.9 = (f32[128,2048]{0,1:T(8,128)S(1)}, f32[128,2048]{0,1:T(8,128)}, u32[]{:S(2)}) copy-start(f32[128,2048]{0,1:T(8,128)} %copy.71) | copy-start | bytes 3145732
  962.7 418.8 %all-reduce.14.cloned.1.call-start = ((), (), s32[]{:S(2)}) async-start(), calls=%async_computation.5 | async-start | bytes 3145728 | tf_op jit(solution)/shard_map/psum | solution.py:15
  1476.5 48.4 %copy-start.2 = (f32[512,512]{1,0:T(8,128)}, f32[512,512]{1,0:T(8,128)S(1)}, u32[]{:S(2)}) copy-start(f32[512,512]{1,0:T(8,128)S(1)} %get-tuple-element.205) | copy-start | bytes 3145732
  1532.1 8.1 copy-start.17
  1532.1 13.0 copy-start.11
  1532.1 13.0 copy-start.12
  1532.1 13.0 copy-start.13
  1545.1 2.5 copy-start.15
  (1 other events, 1.3 us)
Sparse Core Ops, SparseCore 0:
  61.1 99.7 all-gather.1
  173.2 194.9 reduce-scatter.1
  373.3 364.6 all-reduce.9
  741.2 49.3 all-reduce.15
  962.9 366.0 all-reduce.11
  1332.2 49.3 all-reduce.13
where the time goes:
time: 1580 us; the launch traced here: 1570 us
  waiting for transfers between devices  1120 us (71%)
  other arithmetic  314 us (20%)
  matrix products  78.7 us (5%)
  local copies, waits for them, and re-layouts  34.9 us (2%)
  between operations  20 us (1%)
    psum x2, waiting for transfers between devices, per_device(): panel_strip = lax.psum(own_share, ('arc', 'trow'))  728 us
    reduce_scatter x1, waiting for transfers between devices, per_device(): lax.psum_scatter(contract_rows(selected, projected), 'arc', scatter_dimen...  195 us
    another operation x30, other arithmetic, per_device(): lower_factor = jnp.linalg.cholesky(pivot_block)  159 us
    all_gather x1, waiting for transfers between devices, per_device(): gathered = lax.all_gather(projected, 'tcol', axis=1, tiled=True)  99.7 us
    psum x2, waiting for transfers between devices, broadcast(): return lax.psum(block, axis)  96.9 us
    another operation x5, other arithmetic, per_device(): lax.linalg.triangular_solve(lower_factor, row_strip.T, left_side=True, lo...  79.2 us
    another operation x14, matrix products, per_device(): lax.linalg.triangular_solve(lower_factor, panel_strip, left_side=True, lo...  40.7 us
  transfers between devices with their start and end apart: 6, of which 6 were waited for; matrix products, arithmetic and copies ran while one was open for 0% of the time, Pallas kernels for 0%

commit v1 on v0

v1 whole, which is shorter than its diff:
```python
import functools

import jax
import jax.numpy as jnp
from jax import lax
from jax.experimental import pallas as pl
from jax.experimental.pallas import tpu as pltpu
from jax.sharding import PartitionSpec as P

PANEL = 512
PANELS = 2
LEAD = PANEL * PANELS
RIDGE = 0.1
BLOCK = 128
HIGHEST = lax.Precision.HIGHEST
AXES = ("arc", "trow", "tcol")


def spread(value):
    return jnp.broadcast_to(value, (8, 128))


def small_inverse(pivot):
    d = [list(row) for row in pivot]
    low = [[None] * 8 for _ in range(8)]
    root = [None] * 8
    for k in range(8):
        root[k] = lax.rsqrt(d[k][k])
        for i in range(k + 1, 8):
            low[i][k] = d[i][k] * root[k]
        for j in range(k + 1, 8):
            for i in range(j, 8):
                d[i][j] = d[i][j] - low[i][k] * low[j][k]
    inv = [[None] * 8 for _ in range(8)]
    for k in range(8):
        inv[k][k] = root[k]
        for i in range(k + 1, 8):
            acc = low[i][k] * inv[k][k]
            for m in range(k + 1, i):
                acc = acc + low[i][m] * inv[m][k]
            inv[i][k] = -acc * root[i]
    return inv


def inverse_factors(matrices):
    lane = lax.broadcasted_iota(jnp.int32, (8, 128), 1)
    sub = lax.broadcasted_iota(jnp.int32, (8, 128), 0)
    zero = jnp.zeros((8, 128), jnp.float32)
    work = [[m[8 * i : 8 * i + 8, :] for i in range(16)] for m in matrices]
    unit = [
        [jnp.where(lane == sub + 8 * i, 1.0, 0.0).astype(jnp.float32) for i in range(16)]
        for _ in matrices
    ]
    for t in range(16):
        for A, X in zip(work, unit):
            lead = 8 * t
            cols = [spread(A[t][:, lead + k : lead + k + 1]) for k in range(8)]
            pivot = [
                [spread(cols[k][i : i + 1, :]) if k <= i else None for k in range(8)]
                for i in range(8)
            ]
            inv = small_inverse(pivot)
            U, UX = zero, zero
            for k in range(8):
                c = zero
                for i in range(k, 8):
                    c = jnp.where(sub == i, inv[i][k], c)
                U = U + c * spread(A[t][k : k + 1, :])
                UX = UX + c * spread(X[t][k : k + 1, :])
            X[t] = UX
            if t == 15:
                continue
            V, VX = zero, zero
            for m in range(8):
                c = zero
                for k in range(m + 1):
                    c = jnp.where(sub == k, inv[m][k], c)
                V = V + c * spread(U[m : m + 1, :])
                VX = VX + c * spread(UX[m : m + 1, :])
            rows = [spread(V[k : k + 1, :]) for k in range(8)]
            rows_x = [spread(VX[k : k + 1, :]) for k in range(8)]
            for i in range(t + 1, 16):
                cs = [spread(A[i][:, lead + k : lead + k + 1]) for k in range(8)]
                for k in range(8):
                    A[i] = A[i] - cs[k] * rows[k]
                    X[i] = X[i] - cs[k] * rows_x[k]
    return [jnp.concatenate(X, 0) for X in unit]


def basis_kernel(lengths_ref, local_ref, basis_ref):
    arcs = basis_ref.shape[0]
    capacity = basis_ref.shape[2]
    row = lax.broadcasted_iota(jnp.int32, (capacity, BLOCK), 0)
    eye = (
        lax.broadcasted_iota(jnp.int32, (BLOCK, BLOCK), 0)
        == lax.broadcasted_iota(jnp.int32, (BLOCK, BLOCK), 1)
    )
    masked, normals = [], []
    for a in range(arcs):
        block = local_ref[a * capacity : (a + 1) * capacity, :].astype(jnp.float32)
        block = jnp.where(row < lengths_ref[a], block, 0.0)
        half = block.astype(jnp.bfloat16)
        normal = lax.dot_general(
            half, half, (((0,), (0,)), ((), ())), preferred_element_type=jnp.float32
        )
        masked.append(block)
        normals.append(normal + jnp.where(eye, RIDGE, 0.0))
    for a, inverse in enumerate(inverse_factors(normals)):
        basis = lax.dot_general(
            inverse,
            masked[a],
            (((1,), (1,)), ((), ())),
            precision=HIGHEST,
            preferred_element_type=jnp.float32,
        )
        basis_ref[a] = basis.astype(jnp.bfloat16)


def local_basis(local_design, lengths):
    arcs = lengths.shape[0]
    capacity = local_design.shape[0] // arcs
    return pl.pallas_call(
        basis_kernel,
        out_shape=jax.ShapeDtypeStruct((arcs, BLOCK, capacity), jnp.bfloat16),
        in_specs=[
            pl.BlockSpec(memory_space=pltpu.SMEM),
            pl.BlockSpec(memory_space=pltpu.VMEM),
        ],
        out_specs=pl.BlockSpec(memory_space=pltpu.VMEM),
        compiler_params=pltpu.CompilerParams(vmem_limit_bytes=32 * 1024 * 1024),
        cost_estimate=pl.CostEstimate(flops=10**9, bytes_accessed=30_000_000, transcendentals=0),
        name="local_basis",
    )(lengths, local_design)


def lead_kernel(pivot_ref, out_ref):
    size = out_ref.shape[0]
    out_ref[...] = pivot_ref[...]
    blocks = size // BLOCK
    for k in range(blocks):
        here = slice(k * BLOCK, (k + 1) * BLOCK)
        inverse = inverse_factors([out_ref[here, here]])[0]
        lead_row = jnp.dot(
            inverse, out_ref[here, :], precision=HIGHEST, preferred_element_type=jnp.float32
        )
        below = slice((k + 1) * BLOCK, size)
        out_ref[here, :] = lead_row
        out_ref[here, here] = inverse
        if k + 1 < blocks:
            coef = out_ref[here, below]
            out_ref[below, here] = jnp.zeros((size - (k + 1) * BLOCK, BLOCK), jnp.float32)
            out_ref[below, :] = out_ref[below, :] - lax.dot_general(
                coef,
                out_ref[here, :],
                (((0,), (0,)), ((), ())),
                precision=HIGHEST,
                preferred_element_type=jnp.float32,
            )
            out_ref[here, below] = jnp.zeros((BLOCK, size - (k + 1) * BLOCK), jnp.float32)


def lead_inverse(pivot):
    return pl.pallas_call(
        lead_kernel,
        out_shape=jax.ShapeDtypeStruct(pivot.shape, jnp.float32),
        in_specs=[pl.BlockSpec(memory_space=pltpu.VMEM)],
        out_specs=pl.BlockSpec(memory_space=pltpu.VMEM),
        compiler_params=pltpu.CompilerParams(vmem_limit_bytes=48 * 1024 * 1024),
        cost_estimate=pl.CostEstimate(
            flops=80 * 10**9, bytes_accessed=250_000_000, transcendentals=0
        ),
        name="lead_inverse",
    )(pivot)


def project(rows, basis, live):
    arcs, _, capacity = basis.shape
    blocks = rows.reshape(arcs, capacity, rows.shape[1])
    loadings = jnp.einsum(
        "alc,acw->alw", basis, blocks, preferred_element_type=jnp.float32
    ).astype(jnp.bfloat16)
    cleaned = blocks.astype(jnp.float32) - jnp.einsum(
        "alc,alw->acw", basis, loadings, preferred_element_type=jnp.float32
    )
    cleaned = jnp.where(live[:, :, None], cleaned, 0.0)
    return cleaned.astype(jnp.bfloat16).reshape(rows.shape)


def contract_rows(left_rows, right_rows):
    return lax.dot_general(
        left_rows, right_rows, (((0,), (0,)), ((), ())), preferred_element_type=jnp.float32
    )


def per_device(design, local_design, lengths, regularizer):
    row_count, col_width = design.shape
    tile = regularizer.shape[0]
    arc_total = lax.axis_size("arc")
    trow_total = lax.axis_size("trow")
    tcol_total = lax.axis_size("tcol")
    arc = lax.axis_index("arc")
    trow = lax.axis_index("trow")
    tcol = lax.axis_index("tcol")
    arcs_per_col = arc_total // tcol_total
    capacity = row_count // lengths.shape[0]
    share = tile // arc_total

    def device_number(a, r, c):
        return (a * trow_total + r) * tcol_total + c

    def over_arc(step, columns):
        return [
            (device_number(a, r, c), device_number(a ^ step, r, c))
            for a in range(arc_total)
            for r in range(trow_total)
            for c in columns
        ]

    every = range(tcol_total)
    live = jnp.arange(capacity, dtype=jnp.int32)[None, :] < lengths[:, None]

    piece = lax.dynamic_slice_in_dim(
        design.reshape(row_count, arcs_per_col, trow_total, tile), trow, 1, 2
    ).reshape(row_count, arcs_per_col * tile)
    gathered = lax.all_gather(piece, "tcol", axis=0)

    basis = local_basis(local_design, lengths)
    own = project(design, basis, live)

    row_ids = jnp.arange(tile, dtype=jnp.int32)
    lead_rows = trow * tile + row_ids
    lead_reg = jnp.where(arc == 0, regularizer, 0.0)

    lead_cols = jnp.arange(LEAD, dtype=jnp.int32)
    pivot_part = contract_rows(
        lax.dynamic_slice_in_dim(own, trow * tile, tile, 1), own[:, :LEAD]
    ) + jnp.where(lead_rows[:, None] == lead_cols[None, :], lead_reg[:, None], 0.0)

    def scatter_sum(part, columns):
        total = lax.dynamic_slice_in_dim(part, arc * share, share, 0)
        for step in range(1, arc_total):
            piece = lax.dynamic_slice_in_dim(part, (arc ^ step) * share, share, 0)
            total = total + lax.ppermute(piece, AXES, over_arc(step, columns))
        return total

    pivot_share = scatter_sum(pivot_part, [0])
    spread_share = jnp.where(tcol == 0, pivot_share, 0.0)
    for c in range(1, tcol_total):
        spread_share = spread_share + lax.ppermute(
            pivot_share,
            AXES,
            [
                (device_number(a, r, 0), device_number(a, r, c))
                for a in range(arc_total)
                for r in range(trow_total)
            ],
        )

    def natural(gathered_rows):
        return (
            gathered_rows.reshape(arc_total, trow_total, share, gathered_rows.shape[-1])
            .transpose(1, 0, 2, 3)
            .reshape(LEAD, gathered_rows.shape[-1])
        )

    pivot = natural(lax.all_gather(spread_share, ("arc", "trow"), axis=0))
    inverse = lead_inverse(pivot)

    cross = gathered.transpose(1, 0, 2).reshape(row_count, arc_total * tile)
    cross = project(cross, basis, live)

    col_ids = tcol * col_width + jnp.arange(col_width, dtype=jnp.int32)
    strip_part = contract_rows(cross[:, :tile], own) + jnp.where(
        lead_rows[:, None] == col_ids[None, :], lead_reg[:, None], 0.0
    )
    strip_share = scatter_sum(strip_part, every)
    strip = natural(lax.all_gather(strip_share, ("arc", "trow"), axis=0))

    def tile_for(target):
        return contract_rows(lax.dynamic_slice_in_dim(cross, target * tile, tile, 1), own)

    normal = tile_for(arc)
    for step in range(1, arc_total):
        normal = normal + lax.ppermute(
            tile_for(arc ^ step).astype(jnp.bfloat16), AXES, over_arc(step, every)
        ).astype(jnp.float32)
    rows_global = (arc * trow_total + trow) * tile + row_ids
    normal = normal + jnp.where(
        rows_global[:, None] == col_ids[None, :], regularizer[:, None], 0.0
    )

    holder = arc // arcs_per_col
    row_own = lax.dynamic_slice_in_dim(
        strip, ((arc % arcs_per_col) * trow_total + trow) * tile, tile, 1
    )
    row_strip = jnp.where(tcol == holder, row_own, 0.0)
    for step in range(1, tcol_total):
        row_strip = row_strip + lax.ppermute(
            row_own,
            AXES,
            [
                (
                    device_number(a, r, a // arcs_per_col),
                    device_number(a, r, (a // arcs_per_col) ^ step),
                )
                for a in range(arc_total)
                for r in range(trow_total)
            ],
        )

    def factor_of(columns, ids):
        factors = []
        for p in range(PANELS):
            depth = (p + 1) * PANEL
            factor = lax.dot_general(
                columns[:depth],
                inverse[p * PANEL : depth, :depth],
                (((0,), (1,)), ((), ())),
                precision=lax.Precision.HIGH,
                preferred_element_type=jnp.float32,
            )
            factors.append(jnp.where(ids[:, None] >= p * PANEL, factor, 0.0))
        return factors

    col_factors = factor_of(strip, col_ids)
    row_factors = factor_of(row_strip, rows_global)
    for p in range(PANELS):
        normal = normal - lax.dot_general(
            row_factors[p],
            col_factors[p],
            (((1,), (1,)), ((), ())),
            precision=lax.Precision.HIGH,
            preferred_element_type=jnp.float32,
        )
    return normal, jnp.stack(col_factors)


def solution(mesh):
    return jax.shard_map(
        per_device,
        mesh=mesh,
        in_specs=(P("arc", "tcol"), P("arc", None), P("arc"), P(("arc", "trow"))),
        out_specs=(P(("arc", "trow"), "tcol"), P(None, "tcol", None)),
        check_vma=False,
    )
```

time: 1580 us -> 451 us (0.29)
  waiting for transfers between devices: 1120 us -> 186 us
  other arithmetic: 314 us -> 17.4 us
  starting transfers between devices: 0.43 us -> 66.2 us
  Pallas kernels: 0 us -> 65.1 us
  matrix products: 78.7 us -> 62 us
    psum x4 -> x0, waiting for transfers between devices: 825 us -> none  [the longest x2 728 us: per_device(): panel_strip = lax.psum(own_share, ('arc', 'trow'))]
    another operation x45 -> x3, other arithmetic: 295 us -> 12.3 us  [per_device(): return (normal, jnp.stack(col_factors))]
    reduce_scatter x1 -> x0, waiting for transfers between devices: 195 us -> none  [per_device(): lax.psum_scatter(contract_rows(selected, projected), 'arc', scatter_dimen...]
    ppermute x0 -> x27, waiting for transfers between devices: none -> 115 us  [the longest x7 81.4 us: per_device(): lax.ppermute(tile_for(arc ^ step).astype(jnp.bfloat16), AXES, over_arc(st...]
    ppermute x0 -> x27, starting transfers between devices: none -> 65.2 us  [the longest x14 40.9 us: scatter_sum(): total = total + lax.ppermute(piece, AXES, over_arc(step, columns))]
    pallas_call x0 -> x2, Pallas kernels: none -> 65.1 us  [the longest x1 57.5 us: lead_inverse(): pl.pallas_call(lead_kernel, out_shape=jax.ShapeDtypeStruct(pivot.shape, j...]
    another operation x41 -> x0, matrix products: 55.4 us -> none  [the longest x14 40.7 us: per_device(): lax.linalg.triangular_solve(lower_factor, panel_strip, left_side=True, lo...]
    all_gather x1 -> x3, waiting for transfers between devices: 99.7 us -> 70.7 us  [the longest x1 41.1 us: per_device(): strip = natural(lax.all_gather(strip_share, ('arc', 'trow'), axis=0))]
  transfers between devices with their start and end apart: 6 -> 30, of which waited for: 6 -> 12; matrix products, arithmetic and copies ran while one was open for 0% -> 21% of each run, Pallas kernels for 0% -> 15%
where the time goes in v1:
time: 451 us; the launch traced here: 445 us
  waiting for transfers between devices  186 us (41%)
  starting transfers between devices  66.2 us (15%)
  Pallas kernels  65.1 us (14%)
  matrix products  62 us (14%)
  local copies, waits for them, and re-layouts  34.3 us (8%)
  other arithmetic  17.4 us (4%)
  between operations  14.5 us (3%)
    ppermute x7, waiting for transfers between devices, per_device(): lax.ppermute(tile_for(arc ^ step).astype(jnp.bfloat16), AXES, over_arc(st...  81.4 us
    pallas_call x1, Pallas kernels, lead_inverse(): pl.pallas_call(lead_kernel, out_shape=jax.ShapeDtypeStruct(pivot.shape, j...  57.5 us
    all_gather x1, waiting for transfers between devices, per_device(): strip = natural(lax.all_gather(strip_share, ('arc', 'trow'), axis=0))  41.1 us
    ppermute x14, starting transfers between devices, scatter_sum(): total = total + lax.ppermute(piece, AXES, over_arc(step, columns))  40.9 us
    ppermute x14, waiting for transfers between devices, scatter_sum(): total = total + lax.ppermute(piece, AXES, over_arc(step, columns))  32.4 us
    all_gather x1, waiting for transfers between devices, per_device(): pivot = natural(lax.all_gather(spread_share, ('arc', 'trow'), axis=0))  29.6 us
    dot_general x4, matrix products, factor_of(): lax.dot_general(columns[:depth], inverse[p * PANEL:depth, :depth], (((0,)...  24.2 us
    dot_general x10, matrix products, contract_rows(): lax.dot_general(left_rows, right_rows, (((0,), (0,)), ((), ())), preferre...  20.1 us
  transfers between devices with their start and end apart: 30, of which 12 were waited for; matrix products, arithmetic and copies ran while one was open for 21% of the time, Pallas kernels for 15%

profile of v1, /device:TPU:0, one launch (start us, length us, event | category | flops | bytes accessed | tf_op | source)
XLA Modules:
  0.0 445.2 jit_solution(9065088435221990726)
XLA Ops:
  7.2 4.3 reshape.82
  11.6 4.5 %dynamic-slice_reduce_fusion = bf16[640,2,256]{2,1,0:T(2,128)(2,1)S(1)} fusion(bf16[640,2,4,256]{3,2,1,0:T(4,128)(2,1)S(1)} %reshape.82, s32[]{:T(128)S(6)} %select_n.132), kind=kLoop, calls=%fused_computation.30 | loop fusion | bytes 1310724 | tf_op jit(solution)/shard_map/dynamic_slice | solution.py:222
  17.8 7.7 %local_basis.1 = bf16[2,128,320]{2,1,0:T(8,128)(2,1)S(1)} custom-call(s32[2]{0:T(128)S(1)} %copy-done.2, bf16[640,128]{1,0:T(8,128)(2,1)S(1)} %copy-done.3), custom_call_target="tpu_custom_call" | custom-call | flops 1000000000 | bytes 30000000 | tf_op jit(solution)/shard_map/local_basis/pallas_call | solution.py:122
  31.9 5.0 %collective-permute-start.17 = (f32[32,1024]{1,0:T(8,128)S(1)}, f32[32,1024]{1,0:T(8,128)S(1)}, u32[]{:S(2)}, u32[]{:S(2)}) collective-permute-start(f32[32,1024]{1,0:T(8,128)S(1)} %get-tuple-element.11), channel_id=1, source_target_pairs={{0,16},{4,20},{8,24},{12,28},{16,0},{20,4},{24,8},{28,12},{32,48},... | collective-permute-start | bytes 393224 | tf_op jit(solution)/shard_map/ppermute | solution.py:243
  36.9 4.9 %collective-permute-start.23 = (f32[32,1024]{1,0:T(8,128)S(1)}, f32[32,1024]{1,0:T(8,128)S(1)}, u32[]{:S(2)}, u32[]{:S(2)}) collective-permute-start(f32[32,1024]{1,0:T(8,128)S(1)} %get-tuple-element.12), channel_id=1, source_target_pairs={{0,112},{4,116},{8,120},{12,124},{16,96},{20,100},{24,104},{28,108... | collective-permute-start | bytes 393224 | tf_op jit(solution)/shard_map/ppermute | solution.py:243
  43.8 6.4 %collective-permute-start.21 = (f32[32,1024]{1,0:T(8,128)}, f32[32,1024]{1,0:T(8,128)}, u32[]{:S(2)}, u32[]{:S(2)}) collective-permute-start(f32[32,1024]{1,0:T(8,128)} %get-tuple-element.14), channel_id=1, source_target_pairs={{0,80},{4,84},{8,88},{12,92},{16,64},{20,68},{24,72},{28,76},{32,1... | collective-permute-start | bytes 393224 | tf_op jit(solution)/shard_map/ppermute | solution.py:243
  72.1 5.3 %copy.14 = bf16[640,4,512]{2,1,0:T(4,128)(2,1)} copy(bf16[640,4,512]{2,0,1:T(8,128)(2,1)} %bitcast.67) | data formatting | bytes 5242880 | tf_op jit(solution)/shard_map/transpose | solution.py:269
  77.4 5.5 %reshape_reshape.3 = bf16[2,320,2048]{2,1,0:T(8,128)(2,1)} reshape(bf16[640,4,512]{2,1,0:T(4,128)(2,1)} %copy.14) | data formatting | bytes 5242880 | tf_op jit(solution)/shard_map/reshape;reshape | solution.py:178
  82.9 5.5 %select_convert_fusion.1 = bf16[2,320,2048]{2,1,0:T(8,128)(2,1)} fusion(bf16[2,320,2048]{2,1,0:T(8,128)(2,1)} %reshape_reshape.3, bf16[2,128,320]{2,1,0:T(8,128)(2,1)S(1)} %local_basis.1, pred[2,320]{1,0:T(4,128)(4,1)S(1)} %iota_compare_fusion.1), kind=kOutput, calls=%fused_computation.2 | convolution fusion | flops 676855808 | bytes 5407360 | tf_op jit(solution)/shard_map/alc,alw->acw/dot_general | solution.py:182
  103.9 7.6 %collective-permute-done.13 = f32[32,2048]{1,0:T(8,128)S(1)} collective-permute-done((f32[32,2048]{1,0:T(8,128)S(1)}, f32[32,2048]{1,0:T(8,128)S(1)}, u32[]{:S(2)}, u32[]{:S(2)}) %collective-permute-start.13) | collective-permute-done | bytes 262176 | tf_op jit(solution)/shard_map/ppermute | solution.py:243
  111.5 10.9 %collective-permute-done.12 = f32[32,2048]{1,0:T(8,128)S(1)} collective-permute-done((f32[32,2048]{1,0:T(8,128)S(1)}, f32[32,2048]{1,0:T(8,128)S(1)}, u32[]{:S(2)}, u32[]{:S(2)}) %collective-permute-start.12) | collective-permute-done | bytes 262176 | tf_op jit(solution)/shard_map/ppermute | solution.py:243
  122.4 7.0 %collective-permute-done.10 = f32[32,2048]{1,0:T(8,128)S(1)} collective-permute-done((f32[32,2048]{1,0:T(8,128)S(1)}, f32[32,2048]{1,0:T(8,128)S(1)}, u32[]{:S(2)}, u32[]{:S(2)}) %collective-permute-start.10) | collective-permute-done | bytes 262176 | tf_op jit(solution)/shard_map/ppermute | solution.py:243
  152.8 29.6 %all-gather.10.cloned.1.call-done = f32[1024,1024]{1,0:T(8,128)} async-done(((f32[32,1024]{1,0:T(8,128)}), f32[1024,1024]{1,0:T(8,128)}) %all-gather.10.cloned.1.call-update) | async-done | bytes 4194320 | tf_op jit(solution)/shard_map/all_gather | solution.py:266
  182.4 4.8 %copy.20 = f32[8,4,32,1024]{3,2,0,1:T(8,128)} copy(f32[8,4,32,1024]{3,2,1,0:T(8,128)} %bitcast.55) | data formatting | bytes 8388608 | tf_op jit(solution)/shard_map/reshape | solution.py:261
  187.2 57.5 %lead_inverse.1 = f32[1024,1024]{1,0:T(8,128)S(1)} custom-call(f32[1024,1024]{1,0:T(8,128)} %bitcast.56), custom_call_target="tpu_custom_call" | custom-call | flops 80000000000 | bytes 250000000 | tf_op jit(solution)/shard_map/lead_inverse/pallas_call | solution.py:163
  246.7 41.1 %all-gather.8.cloned.1.call-done = f32[1024,2048]{1,0:T(8,128)} async-done(((f32[32,2048]{1,0:T(8,128)}), f32[1024,2048]{1,0:T(8,128)}) %all-gather.8.cloned.1.call-update) | async-done | bytes 8388624 | tf_op jit(solution)/shard_map/all_gather | solution.py:277
  300.3 14.2 %fusion.8 = f32[2048,512]{1,0:T(8,128)S(1)} fusion(f32[1024,2048]{1,0:T(8,128)S(1)} %bitcast.50, f32[1024,1024]{1,0:T(8,128)S(1)} %copy-done.1), kind=kOutput, calls=%fused_computation.24 | convolution fusion | flops 6442450944 | bytes 14680064 | tf_op jit(solution)/shard_map/dot_general | solution.py:315
  315.0 7.0 %fusion.18 = f32[2048,512]{1,0:T(8,128)S(1)} fusion(f32[512,2048]{1,0:T(8,128)S(1)} %bitcast.53, f32[1024,1024]{1,0:T(8,128)S(1)} %copy-done.1), kind=kOutput, calls=%fused_computation.35 | convolution fusion | flops 3221225472 | bytes 9437184 | tf_op jit(solution)/shard_map/dot_general | solution.py:315
  326.4 7.8 %pad_maximum_fusion = f32[2,2048,512]{2,1,0:T(8,128)} fusion(f32[1,2048,512]{2,1,0:T(8,128)} %select_bitcast_fusion, f32[1,2048,512]{2,1,0:T(8,128)} %select_bitcast_fusion.1), kind=kLoop, calls=%fused_computation | loop fusion | flops 2097152 | bytes 16777216 | tf_op jit(solution)/shard_map/stack | solution.py:335
  334.4 5.0 %collective-permute-start.4 = (bf16[256,2048]{1,0:T(8,128)(2,1)}, bf16[256,2048]{1,0:T(8,128)(2,1)S(1)}, u32[]{:S(2)}, u32[]{:S(2)}) collective-permute-start(bf16[256,2048]{1,0:T(8,128)(2,1)} %convolution_convert_fusion.2), channel_id=1, source_target_pairs={{0,80},{1,81},{2,82},{3,83},{4,84},{5,85},{6,86},{7,87},{8,88},{9,... | collective-permute-start | bytes 3145736 | tf_op jit(solution)/shard_map/ppermute | solution.py:284
  351.4 11.7 %collective-permute-done.2 = bf16[256,2048]{1,0:T(8,128)(2,1)S(1)} collective-permute-done((bf16[256,2048]{1,0:T(8,128)(2,1)}, bf16[256,2048]{1,0:T(8,128)(2,1)S(1)}, u32[]{:S(2)}, u32[]{:S(2)}) %collective-permute-start.2) | collective-permute-done | bytes 1048608 | tf_op jit(solution)/shard_map/ppermute | solution.py:284
  363.1 63.2 %collective-permute-done.3 = bf16[256,2048]{1,0:T(8,128)(2,1)S(1)} collective-permute-done((bf16[256,2048]{1,0:T(8,128)(2,1)}, bf16[256,2048]{1,0:T(8,128)(2,1)S(1)}, u32[]{:S(2)}, u32[]{:S(2)}) %collective-permute-start.3) | collective-permute-done | bytes 1048608 | tf_op jit(solution)/shard_map/ppermute | solution.py:284
  426.3 6.5 %collective-permute-done.5 = bf16[256,2048]{1,0:T(8,128)(2,1)S(1)} collective-permute-done((bf16[256,2048]{1,0:T(8,128)(2,1)}, bf16[256,2048]{1,0:T(8,128)(2,1)S(1)}, u32[]{:S(2)}, u32[]{:S(2)}) %collective-permute-start.5) | collective-permute-done | bytes 1048608 | tf_op jit(solution)/shard_map/ppermute | solution.py:284
  432.8 5.7 %subtract_subtract_fusion = f32[256,2048]{1,0:T(8,128)} fusion(f32[256,2048]{1,0:T(8,128)S(1)} %fusion, bf16[256,2048]{1,0:T(8,128)(2,1)S(1)} %collective-permute-done.6, bf16[256,2048]{1,0:T(8,128)(2,1)S(1)} %collective-permute-done.5, bf16[256,2048]{1,0:T(8,128)(2,1)S(1)} %collective-permute-done.4, bf16[256,2048]{1,0:T(8,128)(2,1)S(1)} %collective-permute-done.3, ...), kind=kOutput, calls=%fused_computation.19 | convolution fusion | flops 1621622784 | bytes 18362368 | tf_op jit(solution)/shard_map/dot_general | solution.py:328
  (100 shorter events, 102.2 us)
Async XLA Ops:
  7.2 65.0 %all-gather.6.cloned.1.call-start = ((), (), s32[]{:S(2)}) async-start(), calls=%async_computation | async-start | bytes 3276800 | tf_op jit(solution)/shard_map/all_gather | solution.py:225
  17.3 165.1 %all-gather.10.cloned.1.call-start = ((), (), s32[]{:S(2)}) async-start(), calls=%async_computation.2 | async-start | bytes 4325376 | tf_op jit(solution)/shard_map/all_gather | solution.py:266
  31.9 21.9 %collective-permute-start.17 = (f32[32,1024]{1,0:T(8,128)S(1)}, f32[32,1024]{1,0:T(8,128)S(1)}, u32[]{:S(2)}, u32[]{:S(2)}) collective-permute-start(f32[32,1024]{1,0:T(8,128)S(1)} %get-tuple-element.11), channel_id=1, source_target_pairs={{0,16},{4,20},{8,24},{12,28},{16,0},{20,4},{24,8},{28,12},{32,48},... | collective-permute-start | bytes 393224 | tf_op jit(solution)/shard_map/ppermute | solution.py:243
  36.9 19.1 %collective-permute-start.23 = (f32[32,1024]{1,0:T(8,128)S(1)}, f32[32,1024]{1,0:T(8,128)S(1)}, u32[]{:S(2)}, u32[]{:S(2)}) collective-permute-start(f32[32,1024]{1,0:T(8,128)S(1)} %get-tuple-element.12), channel_id=1, source_target_pairs={{0,112},{4,116},{8,120},{12,124},{16,96},{20,100},{24,104},{28,108... | collective-permute-start | bytes 393224 | tf_op jit(solution)/shard_map/ppermute | solution.py:243
  41.8 17.7 %collective-permute-start.22 = (f32[32,1024]{1,0:T(8,128)}, f32[32,1024]{1,0:T(8,128)S(1)}, u32[]{:S(2)}, u32[]{:S(2)}) collective-permute-start(f32[32,1024]{1,0:T(8,128)} %get-tuple-element.13), channel_id=1, source_target_pairs={{0,96},{4,100},{8,104},{12,108},{16,112},{20,116},{24,120},{28,124... | collective-permute-start | bytes 393224 | tf_op jit(solution)/shard_map/ppermute | solution.py:243
  43.8 15.7 %collective-permute-start.21 = (f32[32,1024]{1,0:T(8,128)}, f32[32,1024]{1,0:T(8,128)}, u32[]{:S(2)}, u32[]{:S(2)}) collective-permute-start(f32[32,1024]{1,0:T(8,128)} %get-tuple-element.14), channel_id=1, source_target_pairs={{0,80},{4,84},{8,88},{12,92},{16,64},{20,68},{24,72},{28,76},{32,1... | collective-permute-start | bytes 393224 | tf_op jit(solution)/shard_map/ppermute | solution.py:243
  71.5 216.3 %all-gather.8.cloned.1.call-start = ((), (), s32[]{:S(2)}) async-start(), calls=%async_computation.1 | async-start | bytes 8650752 | tf_op jit(solution)/shard_map/all_gather | solution.py:277
  90.6 10.8 %collective-permute-start.7 = (f32[32,2048]{1,0:T(8,128)S(1)}, f32[32,2048]{1,0:T(8,128)S(1)}, u32[]{:S(2)}, u32[]{:S(2)}) collective-permute-start(f32[32,2048]{1,0:T(8,128)S(1)} %get-tuple-element.4), channel_id=1, source_target_pairs={{0,16},{1,17},{2,18},{3,19},{4,20},{5,21},{6,22},{7,23},{8,24},{9,... | collective-permute-start | bytes 786440 | tf_op jit(solution)/shard_map/ppermute | solution.py:243
  92.2 19.4 %collective-permute-start.13 = (f32[32,2048]{1,0:T(8,128)S(1)}, f32[32,2048]{1,0:T(8,128)S(1)}, u32[]{:S(2)}, u32[]{:S(2)}) collective-permute-start(f32[32,2048]{1,0:T(8,128)S(1)} %get-tuple-element.5), channel_id=1, source_target_pairs={{0,112},{1,113},{2,114},{3,115},{4,116},{5,117},{6,118},{7,119},{8... | collective-permute-start | bytes 786440 | tf_op jit(solution)/shard_map/ppermute | solution.py:243
  96.3 26.1 %collective-permute-start.12 = (f32[32,2048]{1,0:T(8,128)S(1)}, f32[32,2048]{1,0:T(8,128)S(1)}, u32[]{:S(2)}, u32[]{:S(2)}) collective-permute-start(f32[32,2048]{1,0:T(8,128)S(1)} %get-tuple-element.6), channel_id=1, source_target_pairs={{0,96},{1,97},{2,98},{3,99},{4,100},{5,101},{6,102},{7,103},{8,104... | collective-permute-start | bytes 786440 | tf_op jit(solution)/shard_map/ppermute | solution.py:243
  96.8 25.6 %collective-permute-start.11 = (f32[32,2048]{1,0:T(8,128)S(1)}, f32[32,2048]{1,0:T(8,128)S(1)}, u32[]{:S(2)}, u32[]{:S(2)}) collective-permute-start(f32[32,2048]{1,0:T(8,128)S(1)} %get-tuple-element.7), channel_id=1, source_target_pairs={{0,80},{1,81},{2,82},{3,83},{4,84},{5,85},{6,86},{7,87},{8,88},{9,... | collective-permute-start | bytes 786440 | tf_op jit(solution)/shard_map/ppermute | solution.py:243
  100.7 28.7 %collective-permute-start.10 = (f32[32,2048]{1,0:T(8,128)S(1)}, f32[32,2048]{1,0:T(8,128)S(1)}, u32[]{:S(2)}, u32[]{:S(2)}) collective-permute-start(f32[32,2048]{1,0:T(8,128)S(1)} %get-tuple-element.8), channel_id=1, source_target_pairs={{0,64},{1,65},{2,66},{3,67},{4,68},{5,69},{6,70},{7,71},{8,72},{9,... | collective-permute-start | bytes 786440 | tf_op jit(solution)/shard_map/ppermute | solution.py:243
  101.3 28.0 %collective-permute-start.9 = (f32[32,2048]{1,0:T(8,128)S(1)}, f32[32,2048]{1,0:T(8,128)S(1)}, u32[]{:S(2)}, u32[]{:S(2)}) collective-permute-start(f32[32,2048]{1,0:T(8,128)S(1)} %get-tuple-element.9), channel_id=1, source_target_pairs={{0,48},{1,49},{2,50},{3,51},{4,52},{5,53},{6,54},{7,55},{8,56},{9,... | collective-permute-start | bytes 786440 | tf_op jit(solution)/shard_map/ppermute | solution.py:243
  111.5 19.8 %collective-permute-start.8 = (f32[32,2048]{1,0:T(8,128)S(1)}, f32[32,2048]{1,0:T(8,128)S(1)}, u32[]{:S(2)}, u32[]{:S(2)}) collective-permute-start(f32[32,2048]{1,0:T(8,128)S(1)} %get-tuple-element.10), channel_id=1, source_target_pairs={{0,32},{1,33},{2,34},{3,35},{4,36},{5,37},{6,38},{7,39},{8,40},{9,... | collective-permute-start | bytes 786440 | tf_op jit(solution)/shard_map/ppermute | solution.py:243
  135.5 198.8 %collective-permute-start = (bf16[256,2048]{1,0:T(8,128)(2,1)}, bf16[256,2048]{1,0:T(8,128)(2,1)}, u32[]{:S(2)}, u32[]{:S(2)}) collective-permute-start(bf16[256,2048]{1,0:T(8,128)(2,1)} %convolution_convert_fusion.6), channel_id=1, source_target_pairs={{0,16},{1,17},{2,18},{3,19},{4,20},{5,21},{6,22},{7,23},{8,24},{9,... | collective-permute-start | bytes 3145736 | tf_op jit(solution)/shard_map/ppermute | solution.py:284
  138.6 195.7 %collective-permute-start.1 = (bf16[256,2048]{1,0:T(8,128)(2,1)}, bf16[256,2048]{1,0:T(8,128)(2,1)}, u32[]{:S(2)}, u32[]{:S(2)}) collective-permute-start(bf16[256,2048]{1,0:T(8,128)(2,1)} %convolution_convert_fusion.5), channel_id=1, source_target_pairs={{0,32},{1,33},{2,34},{3,35},{4,36},{5,37},{6,38},{7,39},{8,40},{9,... | collective-permute-start | bytes 3145736 | tf_op jit(solution)/shard_map/ppermute | solution.py:284
  292.1 42.3 %collective-permute-start.15 = (f32[1024,256]{1,0:T(8,128)S(1)}, f32[1024,256]{1,0:T(8,128)}, u32[]{:S(2)}, u32[]{:S(2)}) collective-permute-start(f32[1024,256]{1,0:T(8,128)S(1)} %constant_dynamic-slice_fusion.7), channel_id=1, source_target_pairs={{0,2},{4,6},{8,10},{12,14},{16,18},{20,22},{24,26},{28,30},{33,35}... | collective-permute-start | bytes 3145736 | tf_op jit(solution)/shard_map/ppermute | solution.py:298
  295.5 43.9 %collective-permute-start.14 = (f32[1024,256]{1,0:T(8,128)S(1)}, f32[1024,256]{1,0:T(8,128)}, u32[]{:S(2)}, u32[]{:S(2)}) collective-permute-start(f32[1024,256]{1,0:T(8,128)S(1)} %constant_dynamic-slice_fusion.7), channel_id=1, source_target_pairs={{0,1},{4,5},{8,9},{12,13},{16,17},{20,21},{24,25},{28,29},{33,32},... | collective-permute-start | bytes 3145736 | tf_op jit(solution)/shard_map/ppermute | solution.py:298
  297.8 43.7 %collective-permute-start.16 = (f32[1024,256]{1,0:T(8,128)S(1)}, f32[1024,256]{1,0:T(8,128)}, u32[]{:S(2)}, u32[]{:S(2)}) collective-permute-start(f32[1024,256]{1,0:T(8,128)S(1)} %constant_dynamic-slice_fusion.7), channel_id=1, source_target_pairs={{0,3},{4,7},{8,11},{12,15},{16,19},{20,23},{24,27},{28,31},{33,34}... | collective-permute-start | bytes 3145736 | tf_op jit(solution)/shard_map/ppermute | solution.py:298
  334.3 28.8 %collective-permute-start.2 = (bf16[256,2048]{1,0:T(8,128)(2,1)}, bf16[256,2048]{1,0:T(8,128)(2,1)S(1)}, u32[]{:S(2)}, u32[]{:S(2)}) collective-permute-start(bf16[256,2048]{1,0:T(8,128)(2,1)} %convolution_convert_fusion.4), channel_id=1, source_target_pairs={{0,48},{1,49},{2,50},{3,51},{4,52},{5,53},{6,54},{7,55},{8,56},{9,... | collective-permute-start | bytes 3145736 | tf_op jit(solution)/shard_map/ppermute | solution.py:284
  334.3 92.0 %collective-permute-start.3 = (bf16[256,2048]{1,0:T(8,128)(2,1)}, bf16[256,2048]{1,0:T(8,128)(2,1)S(1)}, u32[]{:S(2)}, u32[]{:S(2)}) collective-permute-start(bf16[256,2048]{1,0:T(8,128)(2,1)} %convolution_convert_fusion.3), channel_id=1, source_target_pairs={{0,64},{1,65},{2,66},{3,67},{4,68},{5,69},{6,70},{7,71},{8,72},{9,... | collective-permute-start | bytes 3145736 | tf_op jit(solution)/shard_map/ppermute | solution.py:284
  334.4 91.9 %collective-permute-start.4 = (bf16[256,2048]{1,0:T(8,128)(2,1)}, bf16[256,2048]{1,0:T(8,128)(2,1)S(1)}, u32[]{:S(2)}, u32[]{:S(2)}) collective-permute-start(bf16[256,2048]{1,0:T(8,128)(2,1)} %convolution_convert_fusion.2), channel_id=1, source_target_pairs={{0,80},{1,81},{2,82},{3,83},{4,84},{5,85},{6,86},{7,87},{8,88},{9,... | collective-permute-start | bytes 3145736 | tf_op jit(solution)/shard_map/ppermute | solution.py:284
  339.4 93.4 %collective-permute-start.5 = (bf16[256,2048]{1,0:T(8,128)(2,1)}, bf16[256,2048]{1,0:T(8,128)(2,1)S(1)}, u32[]{:S(2)}, u32[]{:S(2)}) collective-permute-start(bf16[256,2048]{1,0:T(8,128)(2,1)} %convolution_convert_fusion.1), channel_id=1, source_target_pairs={{0,96},{1,97},{2,98},{3,99},{4,100},{5,101},{6,102},{7,103},{8,104... | collective-permute-start | bytes 3145736 | tf_op jit(solution)/shard_map/ppermute | solution.py:284
  341.5 91.3 %collective-permute-start.6 = (bf16[256,2048]{1,0:T(8,128)(2,1)}, bf16[256,2048]{1,0:T(8,128)(2,1)S(1)}, u32[]{:S(2)}, u32[]{:S(2)}) collective-permute-start(bf16[256,2048]{1,0:T(8,128)(2,1)} %convolution_convert_fusion), channel_id=1, source_target_pairs={{0,112},{1,113},{2,114},{3,115},{4,116},{5,117},{6,118},{7,119},{8... | collective-permute-start | bytes 3145736 | tf_op jit(solution)/shard_map/ppermute | solution.py:284
  (14 other events, 162.9 us)
Sparse Core Ops, SparseCore 0:
  17.5 38.1 all-gather.5
  71.6 110.7 all-gather.9
  185.5 102.2 all-gather.7

commit v2 on v1

v2 whole, which is shorter than its diff:
```python
import jax
import jax.numpy as jnp
from jax import lax
from jax.experimental import pallas as pl
from jax.experimental.pallas import tpu as pltpu
from jax.sharding import PartitionSpec as P

PANEL = 512
PANELS = 2
LEAD = PANEL * PANELS
RIDGE = 0.1
BLOCK = 128
HIGHEST = lax.Precision.HIGHEST
AXES = ("arc", "trow", "tcol")


def spread(value):
    return jnp.broadcast_to(value, (8, 128))


def small_inverse(pivot):
    d = [list(row) for row in pivot]
    low = [[None] * 8 for _ in range(8)]
    root = [None] * 8
    for k in range(8):
        root[k] = lax.rsqrt(d[k][k])
        for i in range(k + 1, 8):
            low[i][k] = d[i][k] * root[k]
        for j in range(k + 1, 8):
            for i in range(j, 8):
                d[i][j] = d[i][j] - low[i][k] * low[j][k]
    inv = [[None] * 8 for _ in range(8)]
    for k in range(8):
        inv[k][k] = root[k]
        for i in range(k + 1, 8):
            acc = low[i][k] * inv[k][k]
            for m in range(k + 1, i):
                acc = acc + low[i][m] * inv[m][k]
            inv[i][k] = -acc * root[i]
    return inv


def inverse_factors(matrices):
    lane = lax.broadcasted_iota(jnp.int32, (8, 128), 1)
    sub = lax.broadcasted_iota(jnp.int32, (8, 128), 0)
    zero = jnp.zeros((8, 128), jnp.float32)
    work = [[m[8 * i : 8 * i + 8, :] for i in range(16)] for m in matrices]
    unit = [
        [jnp.where(lane == sub + 8 * i, 1.0, 0.0).astype(jnp.float32) for i in range(16)]
        for _ in matrices
    ]
    for t in range(16):
        for A, X in zip(work, unit):
            lead = 8 * t
            cols = [spread(A[t][:, lead + k : lead + k + 1]) for k in range(8)]
            pivot = [
                [spread(cols[k][i : i + 1, :]) if k <= i else None for k in range(8)]
                for i in range(8)
            ]
            inv = small_inverse(pivot)
            U, UX = zero, zero
            for k in range(8):
                c = zero
                for i in range(k, 8):
                    c = jnp.where(sub == i, inv[i][k], c)
                U = U + c * spread(A[t][k : k + 1, :])
                UX = UX + c * spread(X[t][k : k + 1, :])
            X[t] = UX
            if t == 15:
                continue
            V, VX = zero, zero
            for m in range(8):
                c = zero
                for k in range(m + 1):
                    c = jnp.where(sub == k, inv[m][k], c)
                V = V + c * spread(U[m : m + 1, :])
                VX = VX + c * spread(UX[m : m + 1, :])
            rows = [spread(V[k : k + 1, :]) for k in range(8)]
            rows_x = [spread(VX[k : k + 1, :]) for k in range(8)]
            for i in range(t + 1, 16):
                cs = [spread(A[i][:, lead + k : lead + k + 1]) for k in range(8)]
                for k in range(8):
                    A[i] = A[i] - cs[k] * rows[k]
                    X[i] = X[i] - cs[k] * rows_x[k]
    return [jnp.concatenate(X, 0) for X in unit]


def basis_kernel(lengths_ref, local_ref, basis_ref):
    arcs = basis_ref.shape[0]
    capacity = basis_ref.shape[2]
    row = lax.broadcasted_iota(jnp.int32, (capacity, BLOCK), 0)
    eye = (
        lax.broadcasted_iota(jnp.int32, (BLOCK, BLOCK), 0)
        == lax.broadcasted_iota(jnp.int32, (BLOCK, BLOCK), 1)
    )
    masked, normals = [], []
    for a in range(arcs):
        block = local_ref[a * capacity : (a + 1) * capacity, :].astype(jnp.float32)
        block = jnp.where(row < lengths_ref[a], block, 0.0)
        half = block.astype(jnp.bfloat16)
        normal = lax.dot_general(
            half, half, (((0,), (0,)), ((), ())), preferred_element_type=jnp.float32
        )
        masked.append(block)
        normals.append(normal + jnp.where(eye, RIDGE, 0.0))
    for a, inverse in enumerate(inverse_factors(normals)):
        basis = lax.dot_general(
            inverse,
            masked[a],
            (((1,), (1,)), ((), ())),
            precision=HIGHEST,
            preferred_element_type=jnp.float32,
        )
        basis_ref[a] = basis.astype(jnp.bfloat16)


def local_basis(local_design, lengths):
    arcs = lengths.shape[0]
    capacity = local_design.shape[0] // arcs
    return pl.pallas_call(
        basis_kernel,
        out_shape=jax.ShapeDtypeStruct((arcs, BLOCK, capacity), jnp.bfloat16),
        in_specs=[
            pl.BlockSpec(memory_space=pltpu.SMEM),
            pl.BlockSpec(memory_space=pltpu.VMEM),
        ],
        out_specs=pl.BlockSpec(memory_space=pltpu.VMEM),
        compiler_params=pltpu.CompilerParams(vmem_limit_bytes=32 * 1024 * 1024),
        cost_estimate=pl.CostEstimate(flops=10**9, bytes_accessed=30_000_000, transcendentals=0),
        name="local_basis",
    )(lengths, local_design)


def mesh_copy(src, dst, send, recv, device):
    return pltpu.make_async_remote_copy(
        src_ref=src,
        dst_ref=dst,
        send_sem=send,
        recv_sem=recv,
        device_id=device,
        device_id_type=pl.DeviceIdType.MESH,
    )


def greet(devices):
    barrier = pltpu.get_barrier_semaphore()
    for device in devices:
        pl.semaphore_signal(
            barrier, inc=1, device_id=device, device_id_type=pl.DeviceIdType.MESH
        )
    pl.semaphore_wait(barrier, len(devices))


def eliminate(out_ref, before):
    size = out_ref.shape[0]
    blocks = size // BLOCK
    col = lax.broadcasted_iota(jnp.int32, (BLOCK, size), 1)

    def step(k, _):
        before(k)
        base = pl.multiple_of(k * BLOCK, BLOCK)
        here = pl.ds(base, BLOCK)
        after = base + BLOCK
        inverse = inverse_factors([out_ref[here, here]])[0]
        out_ref[here, here] = jnp.where(
            lax.broadcasted_iota(jnp.int32, (BLOCK, BLOCK), 0)
            == lax.broadcasted_iota(jnp.int32, (BLOCK, BLOCK), 1),
            1.0,
            0.0,
        )
        lead_row = jnp.dot(
            inverse, out_ref[here, :], precision=HIGHEST, preferred_element_type=jnp.float32
        )
        coef = jnp.where(col >= after, lead_row, 0.0)

        def trail(first):
            below = slice(first, size)
            row = lax.broadcasted_iota(jnp.int32, (size - first, BLOCK), 0) + first
            out_ref[below, here] = jnp.where(row >= after, 0.0, out_ref[below, here])
            out_ref[below, :] = out_ref[below, :] - lax.dot_general(
                coef[:, below],
                lead_row,
                (((0,), (0,)), ((), ())),
                precision=HIGHEST,
                preferred_element_type=jnp.float32,
            )

        half = blocks // 2

        @pl.when(k < half)
        def _():
            trail(BLOCK)

        @pl.when((k >= half) & (k < blocks - 1))
        def _():
            trail((half + 1) * BLOCK)

        out_ref[here, :] = jnp.where(col < after, lead_row, 0.0)
        return 0

    lax.fori_loop(0, blocks, step, 0)


def gather_kernel(
    own, piece, pivot_part, regs, pivot, strip_out, both, cross,
    pivot_in, strip_part, strip_in, chunk, half, stack, total_ref, first, swap_in, pair_sum, pair_in,
    first_send, first_recv, swap_send, swap_recv, mine_send, mine_recv,
    theirs_send, theirs_recv, plane_send, plane_recv,
    part_send, part_recv, half_send, half_recv, stack_send, stack_recv,
    lead_send, lead_recv, core_send, core_recv, strip_send, strip_recv,
    wide_send, wide_recv, relay_send, relay_recv, pair_send, pair_recv, own_sem, local_sem,
):
    trows, arcs, cores, depth, width = pivot.shape
    share = total_ref.shape[0]
    tcols = half_send.shape[0]
    tile = width // trows
    a, r, c = lax.axis_index("arc"), lax.axis_index("trow"), lax.axis_index("tcol")
    core = lax.rem(c, 2)
    parity = lax.rem(a, 2)
    others = range(1, arcs)
    greet(
        [(a ^ m, r, c) for m in others]
        + [(a, r ^ q, c) for q in range(1, trows)]
        + [(a, r, c ^ q) for q in range(1, tcols)]
    )

    def rows_of(part, target):
        return part.at[pl.ds(pl.multiple_of(target * share, share), share)]

    parts = [
        mesh_copy(
            rows_of(pivot_part, a ^ m), pivot_in.at[m],
            part_send.at[m], part_recv.at[m], (a ^ m, r, c),
        )
        for m in others
    ]
    groups = arcs // 2
    beyond = range(1, groups)
    strips = [
        mesh_copy(
            strip_part.at[pl.ds(pl.multiple_of((a // 2 ^ m) * 2 * share, 2 * share), 2 * share)],
            strip_in.at[m],
            strip_send.at[m], strip_recv.at[m], (a ^ (2 * m), r, c),
        )
        for m in beyond
    ]
    firsts = [
        mesh_copy(piece.at[0], first, first_send.at[q], first_recv, (a, r, q))
        for q in range(1, tcols)
    ]
    swap = mesh_copy(piece, swap_in, swap_send, swap_recv, (a ^ 1, r, c))
    mine = [
        mesh_copy(
            piece.at[parity], cross.at[c, 0], mine_send.at[q], mine_recv.at[q], (a, r, c ^ q)
        )
        for q in (1, 2)
    ]
    theirs = [
        mesh_copy(
            swap_in.at[parity], cross.at[c, 1], theirs_send.at[q], theirs_recv.at[q], (a, r, c ^ q)
        )
        for q in (1, 2)
    ]
    relays = [
        mesh_copy(
            cross.at[c ^ 2], cross.at[c ^ 2], relay_send.at[0], relay_recv.at[0], (a, r, c ^ 1)
        )
    ]

    def spot(e):
        return pl.ds(pl.multiple_of((e * trows + r) * tile, tile), tile)

    planes = [
        mesh_copy(
            swap_in.at[e], both.at[1, :, spot(e)],
            plane_send.at[q, e], plane_recv.at[q, e], (a, r ^ q, c),
        )
        for q in range(1, trows)
        for e in range(piece.shape[0])
    ]

    @pl.when(c == 0)
    def _():
        for copy in parts + firsts:
            copy.start()
        first[...] = piece[0]

    swap.start()
    keep_mine = pltpu.make_async_copy(piece.at[parity], cross.at[c, 0], local_sem.at[0])
    keep_mine.start()
    keep_own = pltpu.make_async_copy(own, both.at[0], local_sem.at[4])
    keep_own.start()
    for copy in mine:
        copy.start()

    @pl.when(c != 0)
    def _():
        mesh_copy(piece.at[0], first, first_send.at[0], first_recv, (a, r, c ^ 1)).wait_recv()

    wide = 512
    for j in range(0, own.shape[1], wide):
        strip_part[:, j : j + wide] = lax.dot_general(
            first[...],
            own[:, j : j + wide],
            (((0,), (0,)), ((), ())),
            preferred_element_type=jnp.float32,
        )
    lead = pl.ds(pl.multiple_of(r * tile, tile), tile)
    strip_part[:, lead] = strip_part[:, lead] + regs[...]
    for copy in strips:
        copy.start()

    @pl.when(c == 0)
    def _():
        total = rows_of(pivot_part, a)[...]
        for m, copy in enumerate(parts):
            copy.wait_recv()
            total = total + pivot_in[m + 1]
        chunk[...] = total.reshape(chunk.shape)
        spreads = [
            mesh_copy(chunk.at[q % 2], half, half_send.at[q], half_recv, (a, r, q))
            for q in range(1, tcols)
        ]
        for copy in spreads:
            copy.start()
        half[...] = chunk[0]
        for copy in parts + firsts + spreads:
            copy.wait_send()

    @pl.when(c != 0)
    def _():
        mesh_copy(chunk.at[0], half, half_send.at[0], half_recv, (a, r, c ^ 1)).wait_recv()

    stacked = [
        mesh_copy(half, stack.at[r], stack_send.at[q], stack_recv.at[q], (a, r ^ q, c))
        for q in range(1, trows)
    ]
    for copy in stacked:
        copy.start()
    stack[r] = half[...]
    swap.wait_recv()
    for copy in theirs + planes:
        copy.start()
    keep_theirs = pltpu.make_async_copy(swap_in.at[parity], cross.at[c, 1], local_sem.at[1])
    keep_planes = [
        pltpu.make_async_copy(swap_in.at[e], both.at[1, :, spot(e)], local_sem.at[2 + e])
        for e in range(piece.shape[0])
    ]
    for copy in [keep_theirs] + keep_planes:
        copy.start()
    for copy in stacked:
        copy.wait_recv()

    def columns(t):
        return pl.ds(t * tile, width - t * tile)

    leads = [
        [
            mesh_copy(
                stack.at[t, :, columns(t)], pivot.at[t, a, core, :, columns(t)],
                lead_send.at[m, t], lead_recv.at[m, t], (a ^ m, r, c),
            )
            for m in others
        ]
        for t in range(trows)
    ]
    for group in leads:
        for copy in group:
            copy.start()
    for t in range(trows):
        pivot[t, a, core] = stack[t]

    total = strip_part[pl.ds(pl.multiple_of(a // 2 * 2 * share, 2 * share), 2 * share)]
    for m, copy in enumerate(strips):
        copy.wait_recv()
        total = total + strip_in[m + 1]
    pair_sum[...] = total
    pair = mesh_copy(
        rows_of(pair_sum, 1 - parity), pair_in, pair_send, pair_recv, (a ^ 1, r, c)
    )
    pair.start()
    for copy in mine + theirs:
        copy.wait_recv()
    for copy in relays:
        copy.start()
    pair.wait_recv()
    total_ref[...] = rows_of(pair_sum, parity)[...] + pair_in[...]
    own_copy = pltpu.make_async_copy(total_ref, strip_out.at[a], own_sem)
    own_copy.start()
    wides = [
        mesh_copy(total_ref, strip_out.at[a], wide_send.at[m], wide_recv.at[m], (a ^ m, r, c))
        for m in [1] + [2 * m for m in beyond]
    ]
    for copy in wides:
        copy.start()
    wides[0].wait_recv()
    onward = [
        mesh_copy(
            strip_out.at[a ^ 1], strip_out.at[a ^ 1],
            relay_send.at[m], relay_recv.at[m], (a ^ (2 * m), r, c),
        )
        for m in beyond
    ]
    for copy in onward:
        copy.start()

    swaps = []
    for t in range(trows):
        for copy in leads[t]:
            copy.wait_recv()
        copy = mesh_copy(
            pivot.at[t, :, core, :, columns(t)], pivot.at[t, :, core, :, columns(t)],
            core_send.at[t], core_recv.at[t], (a, r, c ^ 1),
        )
        copy.start()
        swaps.append(copy)
    for copy in swaps + planes + relays + wides[1:] + onward:
        copy.wait()
    for copy in [keep_own, keep_mine, keep_theirs, own_copy] + keep_planes:
        copy.wait()
    sent = [swap, pair, wides[0]] + mine + theirs + stacked + strips
    for copy in sent + [copy for group in leads for copy in group]:
        copy.wait_send()


def gather(own, piece, pivot_part, regs, arcs, trows, tcols):
    tile, width = pivot_part.shape
    rows, columns = own.shape
    share = tile // arcs
    depth = share // 2
    dma = pltpu.SemaphoreType.DMA
    vmem = pl.BlockSpec(memory_space=pltpu.VMEM)
    anywhere = pl.BlockSpec(memory_space=pl.ANY)
    return pl.pallas_call(
        gather_kernel,
        out_shape=(
            jax.ShapeDtypeStruct((trows, arcs, 2, depth, width), jnp.float32),
            jax.ShapeDtypeStruct((arcs, share, columns), jnp.float32),
            jax.ShapeDtypeStruct((2,) + own.shape, own.dtype),
            jax.ShapeDtypeStruct((tcols, 2) + piece.shape[1:], piece.dtype),
        ),
        in_specs=[vmem] * 4,
        out_specs=(vmem, anywhere, anywhere, anywhere),
        scratch_shapes=[
            pltpu.VMEM((arcs, share, width), jnp.float32),
            pltpu.VMEM((tile, columns), jnp.float32),
            pltpu.VMEM((arcs // 2, 2 * share, columns), jnp.float32),
            pltpu.VMEM((2, depth, width), jnp.float32),
            pltpu.VMEM((depth, width), jnp.float32),
            pltpu.VMEM((trows, depth, width), jnp.float32),
            pltpu.VMEM((share, columns), jnp.float32),
            pltpu.VMEM(piece.shape[1:], piece.dtype),
            pltpu.VMEM(piece.shape, piece.dtype),
            pltpu.VMEM((2 * share, columns), jnp.float32),
            pltpu.VMEM((share, columns), jnp.float32),
            dma((tcols,)), dma,
            dma, dma,
            dma((tcols,)), dma((tcols,)),
            dma((tcols,)), dma((tcols,)),
            dma((trows, 2)), dma((trows, 2)),
            dma((arcs,)), dma((arcs,)),
            dma((tcols,)), dma,
            dma((trows,)), dma((trows,)),
            dma((arcs, trows)), dma((arcs, trows)),
            dma((trows,)), dma((trows,)),
            dma((arcs,)), dma((arcs,)),
            dma((arcs,)), dma((arcs,)),
            dma((arcs // 2,)), dma((arcs // 2,)),
            dma, dma,
            dma, dma((5,)),
        ],
        compiler_params=pltpu.CompilerParams(
            collective_id=0, has_side_effects=True, vmem_limit_bytes=40 * 1024 * 1024
        ),
        cost_estimate=pl.CostEstimate(
            flops=40 * 10**9, bytes_accessed=250_000_000, transcendentals=0
        ),
        name="gather",
    )(own, piece, pivot_part, regs)


def lead_kernel(
    pivot, plane, tiles, diagonals, inverse_ref, strip_out, received, diagonals_in, rows_out,
    near_send, near_recv, far_send, far_recv, tile_send, tile_recv, own_sem,
    diagonal_send, diagonal_recv, row_send, row_recv, row_local,
):
    trows, arcs = strip_out.shape[:2]
    groups = tiles.shape[0]
    a, r, c = lax.axis_index("arc"), lax.axis_index("trow"), lax.axis_index("tcol")
    up, down = lax.rem(r + 1, trows), lax.rem(r + trows - 1, trows)
    group = a // 2
    tcols = row_send.shape[1]
    tile = rows_out.shape[-1]
    greet(
        [(a ^ (2 * m), r, c) for m in range(1, groups)]
        + [(a, up, c), (a, down, c)]
        + [(a, r, c ^ q) for q in range(1, tcols)]
    )
    some = arcs // 2
    near = [
        mesh_copy(plane, strip_out.at[r], near_send.at[i], near_recv.at[i], (a, z, c))
        for i, z in enumerate((up, down))
    ]
    far = [
        mesh_copy(
            strip_out.at[z, part], strip_out.at[z, part],
            far_send.at[i], far_recv.at[i], (a, to, c),
        )
        for i, (z, part, to) in enumerate(
            ((down, pl.ds(0, some), up), (up, pl.ds(some, some), down))
        )
    ]
    exchanges = [
        mesh_copy(
            tiles.at[group ^ m], received.at[m - 1],
            tile_send.at[m - 1], tile_recv.at[m - 1], (a ^ (2 * m), r, c),
        )
        for m in range(1, groups)
    ] + [
        mesh_copy(
            diagonals.at[group ^ m], diagonals_in.at[m - 1],
            diagonal_send.at[m - 1], diagonal_recv.at[m - 1], (a ^ (2 * m), r, c),
        )
        for m in range(1, groups)
    ]

    holder = c == group
    spot = pl.ds(pl.multiple_of((lax.rem(a, 2) * trows + r) * tile, tile), tile)
    places = (r, up, down, lax.rem(r + 2, trows))

    def row_copies(i):
        source = (plane if i == 0 else strip_out.at[places[i]]).at[:, :, spot]
        target = rows_out.at[places[i]]
        away = [
            mesh_copy(source, target, row_send.at[i, q], row_recv.at[i], (a, r, c ^ q))
            for q in range(1, tcols)
        ]
        return away, pltpu.make_async_copy(source, target, row_local.at[i])

    def send_rows(i):
        @pl.when(holder)
        def _():
            away, here = row_copies(i)
            for copy in away:
                copy.start()
            here.start()

    send_rows(0)
    for copy in near + exchanges:
        copy.start()
    keep = pltpu.make_async_copy(plane, strip_out.at[r], own_sem)
    keep.start()
    inverse_ref[...] = pivot[...].reshape(inverse_ref.shape)

    def before(k):
        @pl.when(k == 6)
        def _():
            for copy in near:
                copy.wait_recv()
            for copy in far:
                copy.start()
            send_rows(1)
            send_rows(2)

    eliminate(inverse_ref, before)
    for copy in far:
        copy.wait_recv()
    send_rows(3)
    for copy in exchanges:
        copy.wait()

    @pl.when(holder)
    def _():
        for i in range(len(places)):
            away, here = row_copies(i)
            for copy in away:
                copy.wait_send()
            here.wait()

    @pl.when(jnp.logical_not(holder))
    def _():
        for i in range(len(places)):
            row_copies(i)[0][0].wait_recv()

    for copy in far:
        copy.wait_send()
    for copy in near:
        copy.wait_send()
    keep.wait()


def lead(pivot, plane, tiles, diagonals, tcols):
    trows, arcs = pivot.shape[:2]
    width = pivot.shape[-1]
    groups = tiles.shape[0]
    dma = pltpu.SemaphoreType.DMA
    vmem = pl.BlockSpec(memory_space=pltpu.VMEM)
    anywhere = pl.BlockSpec(memory_space=pl.ANY)
    return pl.pallas_call(
        lead_kernel,
        out_shape=(
            jax.ShapeDtypeStruct((width, width), jnp.float32),
            jax.ShapeDtypeStruct((trows,) + plane.shape, jnp.float32),
            jax.ShapeDtypeStruct((groups - 1,) + tiles.shape[1:], tiles.dtype),
            jax.ShapeDtypeStruct((groups - 1,) + diagonals.shape[1:], jnp.float32),
            jax.ShapeDtypeStruct((trows,) + plane.shape[:2] + diagonals.shape[2:], jnp.float32),
        ),
        in_specs=[vmem, anywhere, anywhere, vmem],
        out_specs=(vmem, anywhere, anywhere, vmem, anywhere),
        scratch_shapes=[
            dma((2,)), dma((2,)),
            dma((2,)), dma((2,)),
            dma((groups - 1,)), dma((groups - 1,)),
            dma,
            dma((groups - 1,)), dma((groups - 1,)),
            dma((trows, tcols)), dma((trows,)), dma((trows,)),
        ],
        compiler_params=pltpu.CompilerParams(
            collective_id=1, has_side_effects=True, vmem_limit_bytes=48 * 1024 * 1024
        ),
        cost_estimate=pl.CostEstimate(
            flops=80 * 10**9, bytes_accessed=250_000_000, transcendentals=0
        ),
        name="lead",
    )(pivot, plane, tiles, diagonals)


def halves(value):
    high = value.astype(jnp.bfloat16)
    return high, (value - high.astype(jnp.float32)).astype(jnp.bfloat16)


def factor_kernel(first_ref, strip_ref, high_ref, low_ref, out_ref):
    wide = strip_ref.shape[1]
    column = (
        first_ref[0] + pl.program_id(0) * wide
        + lax.broadcasted_iota(jnp.int32, (wide, PANEL), 0)
    )
    high, low = halves(strip_ref[...])

    def product(left, right):
        return lax.dot_general(
            left, right, (((0,), (0,)), ((), ())), preferred_element_type=jnp.float32
        )

    for p in range(PANELS):
        depth = (p + 1) * PANEL
        panel = slice(p * PANEL, depth)
        factor = (
            product(high[:depth], low_ref[:depth, panel])
            + product(low[:depth], high_ref[:depth, panel])
            + product(high[:depth], high_ref[:depth, panel])
        )
        out_ref[p] = jnp.where(column >= p * PANEL, factor, 0.0)


def panel_factors(strip, high, low, first):
    columns = strip.shape[1]
    wide = min(columns, 512)
    return pl.pallas_call(
        factor_kernel,
        out_shape=jax.ShapeDtypeStruct((PANELS, columns, PANEL), jnp.float32),
        grid=(columns // wide,),
        in_specs=[
            pl.BlockSpec(memory_space=pltpu.SMEM),
            pl.BlockSpec((LEAD, wide), lambda j: (0, j)),
            pl.BlockSpec((LEAD, LEAD), lambda j: (0, 0)),
            pl.BlockSpec((LEAD, LEAD), lambda j: (0, 0)),
        ],
        out_specs=pl.BlockSpec((PANELS, wide, PANEL), lambda j: (0, j, 0)),
        compiler_params=pltpu.CompilerParams(vmem_limit_bytes=48 * 1024 * 1024),
        cost_estimate=pl.CostEstimate(
            flops=10 * 10**9 * columns // 2048, bytes_accessed=columns * 8192, transcendentals=0
        ),
        name="panel_factors",
    )(first.reshape(1), strip, high, low)


def project(rows, basis, live):
    arcs, _, capacity = basis.shape
    blocks = rows.reshape(rows.shape[0], arcs, capacity, rows.shape[2])
    loadings = jnp.einsum(
        "alc,tacw->talw", basis, blocks, preferred_element_type=jnp.float32
    ).astype(jnp.bfloat16)
    cleaned = blocks.astype(jnp.float32) - jnp.einsum(
        "alc,talw->tacw", basis, loadings, preferred_element_type=jnp.float32
    )
    cleaned = jnp.where(live[None, :, :, None], cleaned, 0.0)
    return cleaned.astype(jnp.bfloat16).reshape(rows.shape)


def contract_rows(left_rows, right_rows):
    return lax.dot_general(
        left_rows, right_rows, (((0,), (0,)), ((), ())), preferred_element_type=jnp.float32
    )


def per_device(design, local_design, lengths, regularizer):
    row_count, col_width = design.shape
    tile = regularizer.shape[0]
    arc_total = lax.axis_size("arc")
    trow_total = lax.axis_size("trow")
    tcol_total = lax.axis_size("tcol")
    arc = lax.axis_index("arc")
    trow = lax.axis_index("trow")
    tcol = lax.axis_index("tcol")
    arcs_per_col = arc_total // tcol_total
    capacity = row_count // lengths.shape[0]

    live = jnp.arange(capacity, dtype=jnp.int32)[None, :] < lengths[:, None]

    basis = local_basis(local_design, lengths)
    own = project(design[None], basis, live)[0]
    piece = jnp.stack(
        [
            lax.dynamic_slice_in_dim(own, (e * trow_total + trow) * tile, tile, 1)
            for e in range(arcs_per_col)
        ]
    )

    row_ids = jnp.arange(tile, dtype=jnp.int32)
    col_ids = tcol * col_width + jnp.arange(col_width, dtype=jnp.int32)

    def tile_rows(a):
        return (jnp.asarray(a)[..., None] * trow_total + trow) * tile + row_ids

    lead_rows = trow * tile + row_ids
    lead_reg = jnp.where(arc == 0, regularizer, 0.0)

    lead_cols = jnp.arange(LEAD, dtype=jnp.int32)
    pivot_part = contract_rows(
        lax.dynamic_slice_in_dim(own, trow * tile, tile, 1), own[:, :LEAD]
    ) + jnp.where(lead_rows[:, None] == lead_cols[None, :], lead_reg[:, None], 0.0)

    lead_diagonal = jnp.where(
        (row_ids[:, None] == row_ids[None, :]) & (tcol == 0), lead_reg[:, None], 0.0
    )
    pivot, plane, both, cross = gather(
        own, piece, pivot_part, lead_diagonal, arc_total, trow_total, tcol_total
    )
    both = both.reshape(2 * row_count, col_width)
    cross = cross.reshape(tcol_total, 2 * row_count, tile)

    group = jnp.arange(tcol_total, dtype=jnp.int32)
    square = (col_ids[None, None, :] == tile_rows(2 * group + arc % 2)[:, :, None])
    tiles = jnp.where(
        square, 0.0, jnp.einsum("ynw,nv->ywv", cross, both, preferred_element_type=jnp.float32)
    ).astype(jnp.bfloat16)
    diagonals = jnp.sum(jnp.square(cross.astype(jnp.float32)), axis=1)[:, None, :]
    inverse, strip, received, diagonals_in, row_strip = lead(
        pivot, plane, tiles, diagonals, tcol_total
    )
    strip = strip.reshape(LEAD, col_width)
    row_strip = row_strip.reshape(LEAD, tile)
    normal = contract_rows(lax.dynamic_index_in_dim(cross, arc // 2, 0, False), both)
    normal = normal + jnp.sum(received.astype(jnp.float32), axis=0)
    rows_global = tile_rows(arc)
    diagonal = regularizer + jnp.sum(diagonals_in, axis=0)[0]
    normal = normal + jnp.where(rows_global[:, None] == col_ids[None, :], diagonal[:, None], 0.0)
    turned = inverse.T
    high = lax.reduce_precision(turned, exponent_bits=8, mantissa_bits=7)
    low = (turned - high).astype(jnp.bfloat16)
    high = high.astype(jnp.bfloat16)
    col_factors = panel_factors(strip, high, low, tcol * col_width)
    row_factors = panel_factors(row_strip, high, low, (arc * trow_total + trow) * tile)
    normal = normal - sum(
        lax.dot_general(
            row_factors[p],
            col_factors[p],
            (((1,), (1,)), ((), ())),
            precision=lax.Precision.HIGH,
            preferred_element_type=jnp.float32,
        )
        for p in range(PANELS)
    )
    return normal, col_factors


def solution(mesh):
    return jax.shard_map(
        per_device,
        mesh=mesh,
        in_specs=(P("arc", "tcol"), P("arc", None), P("arc"), P(("arc", "trow"))),
        out_specs=(P(("arc", "trow"), "tcol"), P(None, "tcol", None)),
        check_vma=False,
    )
```

time: 451 us -> 280 us (0.62)
  waiting for transfers between devices: 186 us -> 0 us
  Pallas kernels: 65.1 us -> 226 us
  starting transfers between devices: 66.2 us -> 0 us
  matrix products: 62 us -> 28 us
  local copies, waits for them, and re-layouts: 34.3 us -> 13.1 us
  between operations: 14.5 us -> 0.86 us
  other arithmetic: 17.4 us -> 9.36 us
    pallas_call x1 -> x4, Pallas kernels: 57.5 us -> 219 us  [the longest x1 106 us: lead(): pl.pallas_call(lead_kernel, out_shape=(jax.ShapeDtypeStruct((width, width...]
    ppermute x27 -> x0, waiting for transfers between devices: 115 us -> none  [the longest x7 81.4 us: per_device(): lax.ppermute(tile_for(arc ^ step).astype(jnp.bfloat16), AXES, over_arc(st...]
    all_gather x3 -> x0, waiting for transfers between devices: 70.7 us -> none  [the longest x1 41.1 us: per_device(): strip = natural(lax.all_gather(strip_share, ('arc', 'trow'), axis=0))]
    ppermute x27 -> x0, starting transfers between devices: 65.2 us -> none  [the longest x14 40.9 us: scatter_sum(): total = total + lax.ppermute(piece, AXES, over_arc(step, columns))]
    dot_general x6 -> x2, matrix products: 33.7 us -> 13.7 us  [the longest x1 9.77 us: per_device(): jnp.einsum('ynw,nv->ywv', cross, both, preferred_element_type=jnp.float32)]
    dot_general x10 -> x2, matrix products: 20.1 us -> 6.67 us  [contract_rows(): lax.dot_general(left_rows, right_rows, (((0,), (0,)), ((), ())), preferre...]
    reshape x3 -> x0, local copies, waits for them, and re-layouts: 13.2 us -> none  [the longest x2 8.91 us: natural(): gathered_rows.reshape(arc_total, trow_total, share, gathered_rows.shape[-1])]
    another operation x3 -> x1, other arithmetic: 12.3 us -> 0.06 us  [per_device(): jnp.stack([lax.dynamic_slice_in_dim(own, (e * trow_total + trow) * tile,...]
  transfers between devices with their start and end apart: 30 -> 0, of which waited for: 12 -> 0; matrix products, arithmetic and copies ran while one was open for 21% -> 0% of each run, Pallas kernels for 15% -> 0%
where the time goes in v2:
time: 280 us; the launch traced here: 278 us
  Pallas kernels  226 us (81%)
  matrix products  28 us (10%)
  local copies, waits for them, and re-layouts  13.1 us (5%)
  other arithmetic  9.36 us (3%)
    pallas_call x1, Pallas kernels, lead(): pl.pallas_call(lead_kernel, out_shape=(jax.ShapeDtypeStruct((width, width...  106 us
    pallas_call x1, Pallas kernels, gather(): pl.pallas_call(gather_kernel, out_shape=(jax.ShapeDtypeStruct((trows, arc...  94.6 us
    pallas_call x2, Pallas kernels, panel_factors(): pl.pallas_call(factor_kernel, out_shape=jax.ShapeDtypeStruct((PANELS, col...  17.8 us
    dot_general x1, matrix products, per_device(): jnp.einsum('ynw,nv->ywv', cross, both, preferred_element_type=jnp.float32)  9.77 us
    unnamed x22, local copies, waits for them, and re-layouts  7.68 us
    pallas_call x1, Pallas kernels, local_basis(): pl.pallas_call(basis_kernel, out_shape=jax.ShapeDtypeStruct((arcs, BLOCK,...  7.67 us
    dot_general x2, matrix products, per_device(): lax.dot_general(row_factors[p], col_factors[p], (((1,), (1,)), ((), ())),...  7.61 us
    dot_general x2, matrix products, contract_rows(): lax.dot_general(left_rows, right_rows, (((0,), (0,)), ((), ())), preferre...  6.67 us

profile of v2, /device:TPU:0, one launch (start us, length us, event | category | flops | bytes accessed | tf_op | source)
XLA Modules:
  0.0 277.8 jit_solution(6463837388382283789)
XLA Ops:
  0.7 0.7 broadcast_select_fusion
  1.4 0.7 iota_compare_fusion.2
  2.2 0.7 copy-done.5
  2.8 0.9 copy-done.6
  3.8 7.7 %local_basis.1 = bf16[2,128,320]{2,1,0:T(8,128)(2,1)S(1)} custom-call(s32[2]{0:T(128)S(1)} %copy-done.5, bf16[640,128]{1,0:T(8,128)(2,1)S(1)} %copy-done.6), custom_call_target="tpu_custom_call" | custom-call | flops 1000000000 | bytes 30000000 | tf_op jit(solution)/shard_map/local_basis/pallas_call | solution.py:120
  11.4 0.1 fusion.18.regs
  11.5 3.9 %fusion.2 = bf16[1,2,320,2048]{3,2,1,0:T(8,128)(2,1)S(1)} fusion(bf16[1,2,320,2048]{3,2,1,0:T(8,128)(2,1)} %bitcast.65, bf16[2,128,320]{2,1,0:T(8,128)(2,1)S(1)} %local_basis.1, pred[2,320]{1,0:T(4,128)(4,1)S(1)} %iota_compare_fusion.2, bf16[2,320,2048]{2,1,0:T(8,128)(2,1)} %bitcast.66), kind=kOutput, calls=%fused_computation.7 | convolution fusion | flops 676855808 | bytes 8028800 | tf_op jit(solution)/shard_map/alc,talw->tacw/dot_general | solution.py:685
  15.7 1.3 copy-done.3
  17.0 0.6 convolution_add_fusion.1.pivot_part
  17.6 1.7 copy-done.4
  19.3 94.6 %gather.1 = (f32[4,8,2,16,1024]{4,3,2,1,0:T(8,128)S(1)}, f32[8,32,2048]{2,1,0:T(8,128)S(1)}, bf16[2,640,2048]{2,1,0:T(8,128)(2,1)}, bf16[4,2,640,256]{3,2,1,0:T(8,128)(2,1)S(1)}) custom-call(bf16[640,2048]{1,0:T(8,128)(2,1)S(1)} %bitcast.63, bf16[2,640,256]{2,1,0:T(8,128)(2,1)S(1)} %pad_maximum_fusion.piece, ...), custom_call_target="tpu_custom_call" | custom-call | flops 40000000000 | bytes 250000000 | tf_op jit(solution)/shard_map/gather/pallas_call | solution.py:434
  114.0 2.0 copy-done.7
  116.0 0.5 multiply_reduce_fusion
  116.5 9.8 %fusion.tiles = bf16[4,256,2048]{2,1,0:T(8,128)(2,1)} fusion(s32[4,256]{1,0:T(4,128)S(1)} %iota_add_fusion.1, s32[2048]{0:T(1024)S(1)} %iota_add_fusion, bf16[4,2,640,256]{3,2,1,0:T(8,128)(2,1)S(1)} %get-tuple-element.11, bf16[2,640,2048]{2,1,0:T(8,128)(2,1)} %get-tuple-element.12), kind=kOutput, calls=%fused_computation.1 | convolution fusion | flops 5375000576 | bytes 12070912 | tf_op jit(solution)/shard_map/ynw,nv->ywv/dot_general | solution.py:747
  126.3 106.4 %lead.1 = (f32[1024,1024]{1,0:T(8,128)}, f32[4,8,32,2048]{3,2,1,0:T(8,128)}, bf16[3,256,2048]{2,1,0:T(8,128)(2,1)}, f32[3,1,256]{2,1,0:T(1,128)S(1)}, f32[4,8,32,256]{3,2,1,0:T(8,128)S(1)}) custom-call(f32[4,8,2,16,1024]{4,3,2,1,0:T(8,128)} %copy-done.7, f32[8,32,2048]{2,1,0:T(8,128)S(1)} %get-tuple-element.14.plane, bf16[4,256,2048]{2,1,0:T(8,128)(2,1)} %fusion.tiles, ...), custom_call_target="tpu_custom_call" | custom-call | flops 80000000000 | bytes 250000000 | tf_op jit(solution)/shard_map/lead/pallas_call | solution.py:599
  232.7 1.0 copy-done.1
  233.7 4.0 %convert_reduce_fusion = f32[256,2048]{1,0:T(8,128)} fusion(bf16[3,256,2048]{2,1,0:T(8,128)(2,1)} %get-tuple-element.15), kind=kLoop, calls=%fused_computation.2 | loop fusion | flops 2621440 | bytes 5242880 | tf_op jit(solution)/shard_map/reduce_sum | solution.py:756
  237.8 6.1 %fusion.12 = f32[256,2048]{1,0:T(8,128)} fusion(f32[256,2048]{1,0:T(8,128)} %convert_reduce_fusion, bf16[1280,2048]{1,0:T(8,128)(2,1)} %bitcast.64, f32[256]{0:T(256)S(1)} %add.135, s32[2048]{0:T(1024)S(1)} %iota_add_fusion, s32[256]{0:T(256)S(1)} %iota_add_fusion.2, bf16[4,1280,256]{2,1,0:T(8,128)(2,1)S(1)} %bitcast.59, s32[]{:T(128)S(6)} %select_n.58), kind=kOutput, calls=%fused_computation.19 | convolution fusion | flops 1344274432 | bytes 10102788 | tf_op jit(solution)/shard_map/dot_general | solution.py:693
  243.9 5.3 %copy.8 = f32[1024,1024]{0,1:T(8,128)} copy(f32[1024,1024]{1,0:T(8,128)} %get-tuple-element.18) | data formatting | bytes 8388608 | tf_op jit(solution)/shard_map/lead/pallas_call | solution.py:599
  249.2 3.1 %fusion.5 = (bf16[1024,1024]{1,0:T(8,128)(2,1)S(1)}, bf16[1024,1024]{1,0:T(8,128)(2,1)S(1)}) fusion(f32[1024,1024]{0,1:T(8,128)} %copy.8), kind=kLoop, calls=%fused_computation.11 | loop fusion | flops 4194304 | bytes 8388608 | tf_op jit(solution)/shard_map/convert_element_type | solution.py:762
  252.3 14.6 %panel_factors.3 = f32[2,2048,512]{2,1,0:T(8,128)} custom-call(s32[1]{0:T(128)} %bitcast.17.first_ref, f32[1024,2048]{1,0:T(8,128)} %bitcast.67, bf16[1024,1024]{1,0:T(8,128)(2,1)S(1)} %get-tuple-element.21.high_ref, bf16[1024,1024]{1,0:T(8,128)(2,1)S(1)} %get-tuple-element.20.low_ref), custom_call_target="tpu_custom_call" | custom-call | flops 10000000000 | bytes 16777216 | tf_op jit(solution)/shard_map/panel_factors/pallas_call | solution.py:660
  266.9 3.2 %panel_factors.2 = f32[2,256,512]{2,1,0:T(8,128)S(1)} custom-call(s32[1]{0:T(128)} %bitcast.13.first_ref, f32[1024,256]{1,0:T(8,128)S(1)} %bitcast.60, bf16[1024,1024]{1,0:T(8,128)(2,1)S(1)} %get-tuple-element.21.high_ref, bf16[1024,1024]{1,0:T(8,128)(2,1)} %copy-done), custom_call_target="tpu_custom_call" | custom-call | flops 1250000000 | bytes 2097152 | tf_op jit(solution)/shard_map/panel_factors/pallas_call | solution.py:660
  270.1 4.2 %fusion.6 = f32[256,2048]{1,0:T(8,128)S(1)} fusion(f32[2,2048,512]{2,1,0:T(8,128)} %panel_factors.3, f32[2,256,512]{2,1,0:T(8,128)S(1)} %panel_factors.2), kind=kOutput, calls=%fused_computation.13 | convolution fusion | flops 1610612736 | bytes 6815744 | tf_op jit(solution)/shard_map/dot_general | solution.py:767
  274.4 3.4 %fusion.11 = f32[256,2048]{1,0:T(8,128)} fusion(f32[256,2048]{1,0:T(8,128)S(1)} %copy-done.9, f32[256,2048]{1,0:T(8,128)S(1)} %fusion.6, f32[2,2048,512]{2,1,0:T(8,128)S(1)} %copy-done.8, f32[2,256,512]{2,1,0:T(8,128)S(1)} %panel_factors.2), kind=kOutput, calls=%fused_computation.17 | convolution fusion | flops 1611661312 | bytes 11010048 | tf_op jit(solution)/shard_map/dot_general | solution.py:767
  (26 shorter events, 0.3 us)
Async XLA Ops:
  2.2 0.7 copy-start.5
  2.8 0.9 copy-start.6
  15.5 1.5 copy-start.3
  17.6 1.7 copy-start.4
  114.0 2.0 copy-start.7
  232.7 1.0 copy-start.1
  233.7 4.1 %copy-start.10 = (f32[256]{0:T(256)S(1)}, f32[256]{0:T(256)}, u32[]{:S(2)}) copy-start(f32[256]{0:T(256)} %param.7) | copy-start | bytes 3076
  252.3 14.6 %copy-start = (bf16[1024,1024]{1,0:T(8,128)(2,1)}, bf16[1024,1024]{1,0:T(8,128)(2,1)S(1)}, u32[]{:S(2)}) copy-start(bf16[1024,1024]{1,0:T(8,128)(2,1)S(1)} %get-tuple-element.20.low_ref) | copy-start | bytes 6291460
  252.3 14.6 %copy-start.2 = (f32[4,8,32,256]{3,2,1,0:T(8,128)S(1)}, f32[4,8,32,256]{3,2,1,0:T(8,128)}, u32[]{:S(2)}) copy-start(f32[4,8,32,256]{3,2,1,0:T(8,128)} %copy-done.1) | copy-start | bytes 3145732
  266.9 7.4 %copy-start.8 = (f32[2,2048,512]{2,1,0:T(8,128)S(1)}, f32[2,2048,512]{2,1,0:T(8,128)}, u32[]{:S(2)}) copy-start(f32[2,2048,512]{2,1,0:T(8,128)} %panel_factors.3) | copy-start | bytes 25165828
  270.1 4.3 %copy-start.9 = (f32[256,2048]{1,0:T(8,128)S(1)}, f32[256,2048]{1,0:T(8,128)}, u32[]{:S(2)}) copy-start(f32[256,2048]{1,0:T(8,128)} %fusion.12) | copy-start | bytes 6291460

commit v3 on v2

--- a/solution.py
+++ b/solution.py
@@ -480,12 +480,13 @@
 
 
 def lead_kernel(
-    pivot, plane, tiles, diagonals, inverse_ref, strip_out, received, diagonals_in, rows_out,
+    pivot, plane, cross, both, diagonals, regs, high_ref, low_ref, strip_out, rows_out, normal,
+    inverse_ref, tiles, received, diagonals_in,
     near_send, near_recv, far_send, far_recv, tile_send, tile_recv, own_sem,
     diagonal_send, diagonal_recv, row_send, row_recv, row_local,
 ):
     trows, arcs = strip_out.shape[:2]
-    groups = tiles.shape[0]
+    groups = cross.shape[0]
     a, r, c = lax.axis_index("arc"), lax.axis_index("trow"), lax.axis_index("tcol")
     up, down = lax.rem(r + 1, trows), lax.rem(r + trows - 1, trows)
     group = a // 2
@@ -516,7 +517,8 @@
             tile_send.at[m - 1], tile_recv.at[m - 1], (a ^ (2 * m), r, c),
         )
         for m in range(1, groups)
-    ] + [
+    ]
+    corners = [
         mesh_copy(
             diagonals.at[group ^ m], diagonals_in.at[m - 1],
             diagonal_send.at[m - 1], diagonal_recv.at[m - 1], (a ^ (2 * m), r, c),
@@ -545,15 +547,41 @@
                 copy.start()
             here.start()
 
+    for copy in near + corners:
+        copy.start()
     send_rows(0)
-    for copy in near + exchanges:
-        copy.start()
     keep = pltpu.make_async_copy(plane, strip_out.at[r], own_sem)
     keep.start()
+
+    def product(g):
+        return lax.dot_general(
+            cross[g], both[...], (((0,), (0,)), ((), ())), preferred_element_type=jnp.float32
+        )
+
+    eye = (
+        lax.broadcasted_iota(jnp.int32, (tile, tile), 0)
+        == lax.broadcasted_iota(jnp.int32, (tile, tile), 1)
+    )
+
+    def send_tile(i, _):
+        g = group ^ (i + 1)
+        tiles[g] = product(g).astype(tiles.dtype)
+
+        @pl.when(c == g)
+        def _():
+            square = jnp.where(eye, 0.0, tiles[g, :, spot].astype(jnp.float32))
+            tiles[g, :, spot] = square.astype(tiles.dtype)
+
+        mesh_copy(
+            tiles.at[g], received.at[i], tile_send.at[i], tile_recv.at[i], (a ^ (2 * (i + 1)), r, c)
+        ).start()
+        return 0
+
+    lax.fori_loop(0, groups - 1, send_tile, 0)
     inverse_ref[...] = pivot[...].reshape(inverse_ref.shape)
 
     def before(k):
-        @pl.when(k == 6)
+        @pl.when(k == 5)
         def _():
             for copy in near:
                 copy.wait_recv()
@@ -566,8 +594,24 @@
     for copy in far:
         copy.wait_recv()
     send_rows(3)
-    for copy in exchanges:
+
+    def turn(i, _):
+        here = pl.ds(pl.multiple_of(i * BLOCK, BLOCK), BLOCK)
+        high_ref[:, here], low_ref[:, here] = halves(inverse_ref[here, :].T)
+        return 0
+
+    lax.fori_loop(0, inverse_ref.shape[0] // BLOCK, turn, 0)
+    normal[...] = product(group)
+    for copy in exchanges + corners:
         copy.wait()
+    diagonal = regs[...]
+    for i in range(groups - 1):
+        normal[...] = normal[...] + received[i].astype(jnp.float32)
+        diagonal = diagonal + diagonals_in[i]
+
+    @pl.when(holder)
+    def _():
+        normal[:, spot] = normal[:, spot] + jnp.where(eye, diagonal, 0.0)
 
     @pl.when(holder)
     def _():
@@ -589,40 +633,46 @@
     keep.wait()
 
 
-def lead(pivot, plane, tiles, diagonals, tcols):
+def lead(pivot, plane, cross, both, diagonals, regs):
     trows, arcs = pivot.shape[:2]
     width = pivot.shape[-1]
-    groups = tiles.shape[0]
+    groups, _, tile = cross.shape
+    columns = both.shape[1]
+    half = both.dtype
     dma = pltpu.SemaphoreType.DMA
     vmem = pl.BlockSpec(memory_space=pltpu.VMEM)
     anywhere = pl.BlockSpec(memory_space=pl.ANY)
     return pl.pallas_call(
         lead_kernel,
         out_shape=(
-            jax.ShapeDtypeStruct((width, width), jnp.float32),
+            jax.ShapeDtypeStruct((width, width), half),
+            jax.ShapeDtypeStruct((width, width), half),
             jax.ShapeDtypeStruct((trows,) + plane.shape, jnp.float32),
-            jax.ShapeDtypeStruct((groups - 1,) + tiles.shape[1:], tiles.dtype),
-            jax.ShapeDtypeStruct((groups - 1,) + diagonals.shape[1:], jnp.float32),
-            jax.ShapeDtypeStruct((trows,) + plane.shape[:2] + diagonals.shape[2:], jnp.float32),
+            jax.ShapeDtypeStruct((trows,) + plane.shape[:2] + (tile,), jnp.float32),
+            jax.ShapeDtypeStruct((tile, columns), jnp.float32),
         ),
-        in_specs=[vmem, anywhere, anywhere, vmem],
-        out_specs=(vmem, anywhere, anywhere, vmem, anywhere),
+        in_specs=[vmem, anywhere, vmem, vmem, vmem, vmem],
+        out_specs=(vmem, vmem, anywhere, anywhere, vmem),
         scratch_shapes=[
+            pltpu.VMEM((width, width), jnp.float32),
+            pltpu.VMEM((groups, tile, columns), half),
+            pltpu.VMEM((groups - 1, tile, columns), half),
+            pltpu.VMEM((groups - 1, 1, tile), jnp.float32),
             dma((2,)), dma((2,)),
             dma((2,)), dma((2,)),
             dma((groups - 1,)), dma((groups - 1,)),
             dma,
             dma((groups - 1,)), dma((groups - 1,)),
-            dma((trows, tcols)), dma((trows,)), dma((trows,)),
+            dma((trows, groups)), dma((trows,)), dma((trows,)),
         ],
         compiler_params=pltpu.CompilerParams(
-            collective_id=1, has_side_effects=True, vmem_limit_bytes=48 * 1024 * 1024
+            collective_id=1, has_side_effects=True, vmem_limit_bytes=52 * 1024 * 1024
         ),
         cost_estimate=pl.CostEstimate(
             flops=80 * 10**9, bytes_accessed=250_000_000, transcendentals=0
         ),
         name="lead",
-    )(pivot, plane, tiles, diagonals)
+    )(pivot, plane, cross, both, diagonals, regs)
 
 
 def halves(value):
@@ -630,50 +680,76 @@
     return high, (value - high.astype(jnp.float32)).astype(jnp.bfloat16)
 
 
-def factor_kernel(first_ref, strip_ref, high_ref, low_ref, out_ref):
+def products(left, right, dims):
+    def one(x, y):
+        return lax.dot_general(x, y, (dims, ((), ())), preferred_element_type=jnp.float32)
+
+    return one(left[0], right[1]) + one(left[1], right[0]) + one(left[0], right[0])
+
+
+def finish_kernel(
+    first_ref, strip_ref, high_ref, low_ref, rows_ref, normal_ref, factor_out, normal_out,
+    row_high, row_low,
+):
+    def factors(columns, first):
+        high, low = halves(columns)
+        ids = first + lax.broadcasted_iota(jnp.int32, (columns.shape[1], PANEL), 0)
+        for p in range(PANELS):
+            depth = (p + 1) * PANEL
+            panel = slice(p * PANEL, depth)
+            factor = products(
+                (high[:depth], low[:depth]),
+                (high_ref[:depth, panel], low_ref[:depth, panel]),
+                ((0,), (0,)),
+            )
+            yield jnp.where(ids >= p * PANEL, factor, 0.0)
+
+    @pl.when(pl.program_id(0) == 0)
+    def _():
+        for p, factor in enumerate(factors(rows_ref[...], first_ref[1])):
+            row_high[p], row_low[p] = halves(factor)
+
+    total = normal_ref[...]
     wide = strip_ref.shape[1]
-    column = (
-        first_ref[0] + pl.program_id(0) * wide
-        + lax.broadcasted_iota(jnp.int32, (wide, PANEL), 0)
-    )
-    high, low = halves(strip_ref[...])
-
-    def product(left, right):
-        return lax.dot_general(
-            left, right, (((0,), (0,)), ((), ())), preferred_element_type=jnp.float32
-        )
-
-    for p in range(PANELS):
-        depth = (p + 1) * PANEL
-        panel = slice(p * PANEL, depth)
-        factor = (
-            product(high[:depth], low_ref[:depth, panel])
-            + product(low[:depth], high_ref[:depth, panel])
-            + product(high[:depth], high_ref[:depth, panel])
-        )
-        out_ref[p] = jnp.where(column >= p * PANEL, factor, 0.0)
-
-
-def panel_factors(strip, high, low, first):
+    for p, factor in enumerate(factors(strip_ref[...], first_ref[0] + pl.program_id(0) * wide)):
+        factor_out[p] = factor
+        total = total - products((row_high[p], row_low[p]), halves(factor), ((1,), (1,)))
+    normal_out[...] = total
+
+
+def finish(strip, high, low, rows, normal, first):
     columns = strip.shape[1]
-    wide = min(columns, 512)
+    tile = normal.shape[0]
+    wide = 512
     return pl.pallas_call(
-        factor_kernel,
-        out_shape=jax.ShapeDtypeStruct((PANELS, columns, PANEL), jnp.float32),
+        finish_kernel,
+        out_shape=(
+            jax.ShapeDtypeStruct((PANELS, columns, PANEL), jnp.float32),
+            jax.ShapeDtypeStruct(normal.shape, jnp.float32),
+        ),
         grid=(columns // wide,),
         in_specs=[
             pl.BlockSpec(memory_space=pltpu.SMEM),
             pl.BlockSpec((LEAD, wide), lambda j: (0, j)),
             pl.BlockSpec((LEAD, LEAD), lambda j: (0, 0)),
             pl.BlockSpec((LEAD, LEAD), lambda j: (0, 0)),
+            pl.BlockSpec((LEAD, tile), lambda j: (0, 0)),
+            pl.BlockSpec((tile, wide), lambda j: (0, j)),
         ],
-        out_specs=pl.BlockSpec((PANELS, wide, PANEL), lambda j: (0, j, 0)),
-        compiler_params=pltpu.CompilerParams(vmem_limit_bytes=48 * 1024 * 1024),
+        out_specs=(
+            pl.BlockSpec((PANELS, wide, PANEL), lambda j: (0, j, 0)),
+            pl.BlockSpec((tile, wide), lambda j: (0, j)),
+        ),
+        scratch_shapes=[
+            pltpu.VMEM((PANELS, tile, PANEL), jnp.bfloat16),
+            pltpu.VMEM((PANELS, tile, PANEL), jnp.bfloat16),
+        ],
+        compiler_params=pltpu.CompilerParams(vmem_limit_bytes=52 * 1024 * 1024),
         cost_estimate=pl.CostEstimate(
-            flops=10 * 10**9 * columns // 2048, bytes_accessed=columns * 8192, transcendentals=0
+            flops=14 * 10**9, bytes_accessed=25_000_000, transcendentals=0
         ),
-        name="panel_factors",
-    )(first.reshape(1), strip, high, low)
+        name="finish",
+    )(first, strip, high, low, rows, normal)
 
 
 def project(rows, basis, live):
@@ -719,11 +795,6 @@
     )
 
     row_ids = jnp.arange(tile, dtype=jnp.int32)
-    col_ids = tcol * col_width + jnp.arange(col_width, dtype=jnp.int32)
-
-    def tile_rows(a):
-        return (jnp.asarray(a)[..., None] * trow_total + trow) * tile + row_ids
-
     lead_rows = trow * tile + row_ids
     lead_reg = jnp.where(arc == 0, regularizer, 0.0)
 
@@ -741,39 +812,15 @@
     both = both.reshape(2 * row_count, col_width)
     cross = cross.reshape(tcol_total, 2 * row_count, tile)
 
-    group = jnp.arange(tcol_total, dtype=jnp.int32)
-    square = (col_ids[None, None, :] == tile_rows(2 * group + arc % 2)[:, :, None])
-    tiles = jnp.where(
-        square, 0.0, jnp.einsum("ynw,nv->ywv", cross, both, preferred_element_type=jnp.float32)
-    ).astype(jnp.bfloat16)
     diagonals = jnp.sum(jnp.square(cross.astype(jnp.float32)), axis=1)[:, None, :]
-    inverse, strip, received, diagonals_in, row_strip = lead(
-        pivot, plane, tiles, diagonals, tcol_total
-    )
-    strip = strip.reshape(LEAD, col_width)
-    row_strip = row_strip.reshape(LEAD, tile)
-    normal = contract_rows(lax.dynamic_index_in_dim(cross, arc // 2, 0, False), both)
-    normal = normal + jnp.sum(received.astype(jnp.float32), axis=0)
-    rows_global = tile_rows(arc)
-    diagonal = regularizer + jnp.sum(diagonals_in, axis=0)[0]
-    normal = normal + jnp.where(rows_global[:, None] == col_ids[None, :], diagonal[:, None], 0.0)
-    turned = inverse.T
-    high = lax.reduce_precision(turned, exponent_bits=8, mantissa_bits=7)
-    low = (turned - high).astype(jnp.bfloat16)
-    high = high.astype(jnp.bfloat16)
-    col_factors = panel_factors(strip, high, low, tcol * col_width)
-    row_factors = panel_factors(row_strip, high, low, (arc * trow_total + trow) * tile)
-    normal = normal - sum(
-        lax.dot_general(
-            row_factors[p],
-            col_factors[p],
-            (((1,), (1,)), ((), ())),
-            precision=lax.Precision.HIGH,
-            preferred_element_type=jnp.float32,
-        )
-        for p in range(PANELS)
-    )
-    return normal, col_factors
+    high, low, strip, row_strip, normal = lead(
+        pivot, plane, cross, both, diagonals, regularizer[None, :]
+    )
+    first = jnp.stack([tcol * col_width, (arc * trow_total + trow) * tile])
+    factors, normal = finish(
+        strip.reshape(LEAD, col_width), high, low, row_strip.reshape(LEAD, tile), normal, first
+    )
+    return normal, factors
 
 
 def solution(mesh):

time: 280 us -> 245 us (0.88)
  matrix products: 28 us -> 4.57 us
  other arithmetic: 9.36 us -> 2.17 us
  local copies, waits for them, and re-layouts: 13.1 us -> 5.93 us
  Pallas kernels: 226 us -> 230 us
    dot_general x3 -> x0, matrix products: 17.4 us -> none  [the longest x1 9.77 us: per_device(): jnp.einsum('ynw,nv->ywv', cross, both, preferred_element_type=jnp.float32)]
    dot_general x2 -> x1, matrix products: 6.67 us -> 0.62 us  [contract_rows(): lax.dot_general(left_rows, right_rows, (((0,), (0,)), ((), ())), preferre...]
    pallas_call x1 -> x0, local copies, waits for them, and re-layouts: 5.34 us -> none  [lead(): pl.pallas_call(lead_kernel, out_shape=(jax.ShapeDtypeStruct((width, width...]
    reduce_sum x2 -> x0, other arithmetic: 4.07 us -> none  [the longest x1 4.05 us: per_device(): normal = normal + jnp.sum(received.astype(jnp.float32), axis=0)]
    pallas_call x2 -> x1, Pallas kernels: 17.8 us -> 21.1 us  [finish(): pl.pallas_call(finish_kernel, out_shape=(jax.ShapeDtypeStruct((PANELS, co...]
    convert_element_type x1 -> x0, other arithmetic: 3.1 us -> none  [per_device(): low = (turned - high).astype(jnp.bfloat16)]
    unnamed x22 -> x12, local copies, waits for them, and re-layouts: 7.68 us -> 5.83 us
where the time goes in v3:
time: 245 us; the launch traced here: 244 us
  Pallas kernels  230 us (94%)
  local copies, waits for them, and re-layouts  5.93 us (2%)
  matrix products  4.57 us (2%)
    pallas_call x1, Pallas kernels, lead(): pl.pallas_call(lead_kernel, out_shape=(jax.ShapeDtypeStruct((width, width...  107 us
    pallas_call x1, Pallas kernels, gather(): pl.pallas_call(gather_kernel, out_shape=(jax.ShapeDtypeStruct((trows, arc...  94.8 us
    pallas_call x1, Pallas kernels, finish(): pl.pallas_call(finish_kernel, out_shape=(jax.ShapeDtypeStruct((PANELS, co...  21.1 us
    pallas_call x1, Pallas kernels, local_basis(): pl.pallas_call(basis_kernel, out_shape=jax.ShapeDtypeStruct((arcs, BLOCK,...  7.67 us
    unnamed x12, local copies, waits for them, and re-layouts  5.83 us

profile of v3, /device:TPU:0, one launch (start us, length us, event | category | flops | bytes accessed | tf_op | source)
XLA Modules:
  0.0 243.8 jit_solution(3229584178612216365)
XLA Ops:
  0.6 0.1 pad_add_fusion.first_ref
  0.7 0.7 broadcast_select_fusion
  1.4 0.7 iota_compare_fusion.2
  2.1 0.0 copy-start.2
  2.1 0.7 copy-done.2
  2.8 0.0 copy-start.3
  2.8 0.9 copy-done.3
  3.7 7.7 %local_basis.1 = bf16[2,128,320]{2,1,0:T(8,128)(2,1)S(1)} custom-call(s32[2]{0:T(128)S(1)} %copy-done.2, bf16[640,128]{1,0:T(8,128)(2,1)S(1)} %copy-done.3), custom_call_target="tpu_custom_call" | custom-call | flops 1000000000 | bytes 30000000 | tf_op jit(solution)/shard_map/local_basis/pallas_call | solution.py:120
  11.4 0.1 fusion.5.regs
  11.5 4.0 %fusion.1 = bf16[1,2,320,2048]{3,2,1,0:T(8,128)(2,1)S(1)} fusion(bf16[1,2,320,2048]{3,2,1,0:T(8,128)(2,1)} %bitcast.32, bf16[2,128,320]{2,1,0:T(8,128)(2,1)S(1)} %local_basis.1, pred[2,320]{1,0:T(4,128)(4,1)S(1)} %iota_compare_fusion.2, bf16[2,320,2048]{2,1,0:T(8,128)(2,1)} %bitcast.33), kind=kOutput, calls=%fused_computation.2 | convolution fusion | flops 676855808 | bytes 8028800 | tf_op jit(solution)/shard_map/alc,talw->tacw/dot_general | solution.py:761
  15.4 0.1 dynamic-slice_bitcast_fusion.1
  15.6 0.1 pad_maximum_fusion.piece
  15.6 0.6 convolution_add_fusion.pivot_part
  16.3 94.8 %gather.1 = (f32[4,8,2,16,1024]{4,3,2,1,0:T(8,128)S(1)}, f32[8,32,2048]{2,1,0:T(8,128)S(1)}, bf16[2,640,2048]{2,1,0:T(8,128)(2,1)}, bf16[4,2,640,256]{3,2,1,0:T(8,128)(2,1)S(1)}) custom-call(bf16[640,2048]{1,0:T(8,128)(2,1)S(1)} %bitcast.29, bf16[2,640,256]{2,1,0:T(8,128)(2,1)S(1)} %pad_maximum_fusion.piece, f32[256,1024]{1,0:T(8,128)S(1)} %convolution_add_fusion.pivot_part, ...), custom_call_target="tpu_custom_call" | custom-call | flops 40000000000 | bytes 250000000 | tf_op jit(solution)/shard_map/gather/pallas_call | solution.py:434
  111.0 0.0 copy-start.4
  111.0 2.0 copy-done.4
  113.0 0.0 copy-start.5
  113.0 1.3 copy-done.5
  114.4 0.0 copy-start
  114.4 0.5 multiply_reduce_fusion
  114.9 0.9 copy-done
  115.8 0.0 copy-done.1
  115.8 106.9 %lead.1 = (bf16[1024,1024]{1,0:T(8,128)(2,1)}, bf16[1024,1024]{1,0:T(8,128)(2,1)}, f32[4,8,32,2048]{3,2,1,0:T(8,128)}, f32[4,8,32,256]{3,2,1,0:T(8,128)S(1)}, f32[256,2048]{1,0:T(8,128)}) custom-call(f32[4,8,2,16,1024]{4,3,2,1,0:T(8,128)} %copy-done.4, f32[8,32,2048]{2,1,0:T(8,128)} %copy-done.5, bf16[4,1280,256]{2,1,0:T(8,128)(2,1)} %bitcast.26, ...), custom_call_target="tpu_custom_call" | custom-call | flops 80000000000 | bytes 250000000 | tf_op jit(solution)/shard_map/lead/pallas_call | solution.py:645
  222.7 21.1 %finish.1 = (f32[2,2048,512]{2,1,0:T(8,128)}, f32[256,2048]{1,0:T(8,128)}) custom-call(s32[2]{0:T(128)S(1)} %pad_add_fusion.first_ref, f32[1024,2048]{1,0:T(8,128)} %bitcast.34, bf16[1024,1024]{1,0:T(8,128)(2,1)} %get-tuple-element.18.high_ref, bf16[1024,1024]{1,0:T(8,128)(2,1)} %get-tuple-element.19.low_ref, f32[1024,256]{1,0:T(8,128)S(1)} %bitcast.31, ...), custom_call_target="tpu_custom_call" | custom-call | flops 14000000000 | bytes 25000000 | tf_op jit(solution)/shard_map/finish/pallas_call | solution.py:724
  (3 shorter events, 0.0 us)
Async XLA Ops:
  2.1 0.7 copy-start.2
  2.8 0.9 copy-start.3
  111.0 2.0 copy-start.4
  113.0 1.3 copy-start.5
  114.4 1.5 copy-start
  114.4 1.5 copy-start.1

commit v4 on v3

--- a/solution.py
+++ b/solution.py
@@ -246,8 +246,9 @@
     ]
     firsts = [
         mesh_copy(piece.at[0], first, first_send.at[q], first_recv, (a, r, q))
-        for q in range(1, tcols)
-    ]
+        for q in (1, 2)
+    ]
+    first_on = mesh_copy(first, first, first_send.at[3], first_recv, (a, r, c ^ 1))
     swap = mesh_copy(piece, swap_in, swap_send, swap_recv, (a ^ 1, r, c))
     mine = [
         mesh_copy(
@@ -281,21 +282,25 @@
 
     @pl.when(c == 0)
     def _():
-        for copy in parts + firsts:
+        for copy in firsts + parts:
             copy.start()
         first[...] = piece[0]
+        for copy in firsts:
+            copy.wait_send()
+
+    @pl.when(c != 0)
+    def _():
+        first_on.wait_recv()
+
+    @pl.when(c == 2)
+    def _():
+        first_on.start()
 
     swap.start()
     keep_mine = pltpu.make_async_copy(piece.at[parity], cross.at[c, 0], local_sem.at[0])
     keep_mine.start()
     keep_own = pltpu.make_async_copy(own, both.at[0], local_sem.at[4])
     keep_own.start()
-    for copy in mine:
-        copy.start()
-
-    @pl.when(c != 0)
-    def _():
-        mesh_copy(piece.at[0], first, first_send.at[0], first_recv, (a, r, c ^ 1)).wait_recv()
 
     wide = 512
     for j in range(0, own.shape[1], wide):
@@ -324,22 +329,26 @@
         for copy in spreads:
             copy.start()
         half[...] = chunk[0]
-        for copy in parts + firsts + spreads:
+        for copy in parts + spreads:
             copy.wait_send()
 
     @pl.when(c != 0)
     def _():
         mesh_copy(chunk.at[0], half, half_send.at[0], half_recv, (a, r, c ^ 1)).wait_recv()
 
+    @pl.when(c == 2)
+    def _():
+        first_on.wait_send()
+
     stacked = [
-        mesh_copy(half, stack.at[r], stack_send.at[q], stack_recv.at[q], (a, r ^ q, c))
-        for q in range(1, trows)
+        mesh_copy(half, stack.at[a], stack_send.at[m], stack_recv.at[m], (a ^ m, r, c))
+        for m in others
     ]
     for copy in stacked:
         copy.start()
-    stack[r] = half[...]
+    stack[a] = half[...]
     swap.wait_recv()
-    for copy in theirs + planes:
+    for copy in planes + mine + theirs:
         copy.start()
     keep_theirs = pltpu.make_async_copy(swap_in.at[parity], cross.at[c, 1], local_sem.at[1])
     keep_planes = [
@@ -351,24 +360,25 @@
     for copy in stacked:
         copy.wait_recv()
 
-    def columns(t):
-        return pl.ds(t * tile, width - t * tile)
-
-    leads = [
-        [
-            mesh_copy(
-                stack.at[t, :, columns(t)], pivot.at[t, a, core, :, columns(t)],
-                lead_send.at[m, t], lead_recv.at[m, t], (a ^ m, r, c),
-            )
-            for m in others
-        ]
-        for t in range(trows)
-    ]
-    for group in leads:
-        for copy in group:
-            copy.start()
-    for t in range(trows):
-        pivot[t, a, core] = stack[t]
+    def lead_copy(t, q, j, to):
+        columns = pl.ds(j * tile, tile)
+        return mesh_copy(
+            stack.at[:, :, columns], pivot.at[t, :, core, :, columns],
+            lead_send.at[q, j], lead_recv.at[q, j], (a, to, c),
+        )
+
+    def leads(act):
+        for q in range(1, trows):
+            for j in range(trows):
+                act(q, j)
+
+    def send_lead(q, j):
+        @pl.when(j >= r)
+        def _():
+            lead_copy(r, q, j, r ^ q).start()
+
+    leads(send_lead)
+    pivot[r, :, core] = stack[...]
 
     total = strip_part[pl.ds(pl.multiple_of(a // 2 * 2 * share, 2 * share), 2 * share)]
     for m, copy in enumerate(strips):
@@ -405,21 +415,32 @@
         copy.start()
 
     swaps = []
-    for t in range(trows):
-        for copy in leads[t]:
-            copy.wait_recv()
+    for q in range(trows):
+        t = r ^ q
+        for j in range(trows if q else 0):
+            @pl.when(j >= t)
+            def _():
+                lead_copy(t, q, j, t).wait_recv()
+
         copy = mesh_copy(
-            pivot.at[t, :, core, :, columns(t)], pivot.at[t, :, core, :, columns(t)],
-            core_send.at[t], core_recv.at[t], (a, r, c ^ 1),
+            pivot.at[t, :, core], pivot.at[t, :, core],
+            core_send.at[q], core_recv.at[q], (a, r, c ^ 1),
         )
         copy.start()
         swaps.append(copy)
+
+    def wait_lead(q, j):
+        @pl.when(j >= r)
+        def _():
+            lead_copy(r, q, j, r ^ q).wait_send()
+
+    leads(wait_lead)
     for copy in swaps + planes + relays + wides[1:] + onward:
         copy.wait()
     for copy in [keep_own, keep_mine, keep_theirs, own_copy] + keep_planes:
         copy.wait()
     sent = [swap, pair, wides[0]] + mine + theirs + stacked + strips
-    for copy in sent + [copy for group in leads for copy in group]:
+    for copy in sent:
         copy.wait_send()
 
 
@@ -447,7 +468,7 @@
             pltpu.VMEM((arcs // 2, 2 * share, columns), jnp.float32),
             pltpu.VMEM((2, depth, width), jnp.float32),
             pltpu.VMEM((depth, width), jnp.float32),
-            pltpu.VMEM((trows, depth, width), jnp.float32),
+            pltpu.VMEM((arcs, depth, width), jnp.float32),
             pltpu.VMEM((share, columns), jnp.float32),
             pltpu.VMEM(piece.shape[1:], piece.dtype),
             pltpu.VMEM(piece.shape, piece.dtype),
@@ -460,8 +481,8 @@
             dma((trows, 2)), dma((trows, 2)),
             dma((arcs,)), dma((arcs,)),
             dma((tcols,)), dma,
-            dma((trows,)), dma((trows,)),
-            dma((arcs, trows)), dma((arcs, trows)),
+            dma((arcs,)), dma((arcs,)),
+            dma((trows, trows)), dma((trows, trows)),
             dma((trows,)), dma((trows,)),
             dma((arcs,)), dma((arcs,)),
             dma((arcs,)), dma((arcs,)),

time: 245 us -> 224 us (0.914)
  Pallas kernels: 230 us -> 207 us
    pallas_call x1, Pallas kernels: 107 us -> 95 us  [lead(): pl.pallas_call(lead_kernel, out_shape=(jax.ShapeDtypeStruct((width, width...]
    pallas_call x1, Pallas kernels: 94.8 us -> 83.7 us  [gather(): pl.pallas_call(gather_kernel, out_shape=(jax.ShapeDtypeStruct((trows, arc...]
where the time goes in v4:
time: 224 us; the launch traced here: 221 us
  Pallas kernels  207 us (92%)
  local copies, waits for them, and re-layouts  5.93 us (3%)
  matrix products  4.57 us (2%)
    pallas_call x1, Pallas kernels, lead(): pl.pallas_call(lead_kernel, out_shape=(jax.ShapeDtypeStruct((width, width...  95 us
    pallas_call x1, Pallas kernels, gather(): pl.pallas_call(gather_kernel, out_shape=(jax.ShapeDtypeStruct((trows, arc...  83.7 us
    pallas_call x1, Pallas kernels, finish(): pl.pallas_call(finish_kernel, out_shape=(jax.ShapeDtypeStruct((PANELS, co...  21.1 us
    pallas_call x1, Pallas kernels, local_basis(): pl.pallas_call(basis_kernel, out_shape=jax.ShapeDtypeStruct((arcs, BLOCK,...  7.67 us
    unnamed x12, local copies, waits for them, and re-layouts  5.83 us

profile of v4, /device:TPU:0, one launch (start us, length us, event | category | flops | bytes accessed | tf_op | source)
XLA Modules:
  0.0 220.9 jit_solution(13564186091448088784)
XLA Ops:
  0.6 0.1 pad_add_fusion.first_ref
  0.7 0.7 broadcast_select_fusion
  1.4 0.7 iota_compare_fusion.2
  2.1 0.0 copy-start.2
  2.1 0.7 copy-done.2
  2.8 0.0 copy-start.3
  2.8 0.9 copy-done.3
  3.7 7.7 %local_basis.1 = bf16[2,128,320]{2,1,0:T(8,128)(2,1)S(1)} custom-call(s32[2]{0:T(128)S(1)} %copy-done.2, bf16[640,128]{1,0:T(8,128)(2,1)S(1)} %copy-done.3), custom_call_target="tpu_custom_call" | custom-call | flops 1000000000 | bytes 30000000 | tf_op jit(solution)/shard_map/local_basis/pallas_call | solution.py:120
  11.4 0.1 fusion.5.regs
  11.5 4.0 %fusion.1 = bf16[1,2,320,2048]{3,2,1,0:T(8,128)(2,1)S(1)} fusion(bf16[1,2,320,2048]{3,2,1,0:T(8,128)(2,1)} %bitcast.32, bf16[2,128,320]{2,1,0:T(8,128)(2,1)S(1)} %local_basis.1, pred[2,320]{1,0:T(4,128)(4,1)S(1)} %iota_compare_fusion.2, bf16[2,320,2048]{2,1,0:T(8,128)(2,1)} %bitcast.33), kind=kOutput, calls=%fused_computation.2 | convolution fusion | flops 676855808 | bytes 8028800 | tf_op jit(solution)/shard_map/alc,talw->tacw/dot_general | solution.py:782
  15.4 0.1 dynamic-slice_bitcast_fusion.1
  15.6 0.1 pad_maximum_fusion.piece
  15.6 0.6 convolution_add_fusion.pivot_part
  16.3 83.7 %gather.1 = (f32[4,8,2,16,1024]{4,3,2,1,0:T(8,128)S(1)}, f32[8,32,2048]{2,1,0:T(8,128)S(1)}, bf16[2,640,2048]{2,1,0:T(8,128)(2,1)}, bf16[4,2,640,256]{3,2,1,0:T(8,128)(2,1)S(1)}) custom-call(bf16[640,2048]{1,0:T(8,128)(2,1)S(1)} %bitcast.29, bf16[2,640,256]{2,1,0:T(8,128)(2,1)S(1)} %pad_maximum_fusion.piece, f32[256,1024]{1,0:T(8,128)S(1)} %convolution_add_fusion.pivot_part, ...), custom_call_target="tpu_custom_call" | custom-call | flops 40000000000 | bytes 250000000 | tf_op jit(solution)/shard_map/gather/pallas_call | solution.py:455
  100.0 0.0 copy-start.4
  100.0 2.0 copy-done.4
  102.0 0.0 copy-start.5
  102.0 1.3 copy-done.5
  103.3 0.0 copy-start
  103.3 0.5 multiply_reduce_fusion
  103.8 0.9 copy-done
  104.8 0.0 copy-done.1
  104.8 95.0 %lead.1 = (bf16[1024,1024]{1,0:T(8,128)(2,1)}, bf16[1024,1024]{1,0:T(8,128)(2,1)}, f32[4,8,32,2048]{3,2,1,0:T(8,128)}, f32[4,8,32,256]{3,2,1,0:T(8,128)S(1)}, f32[256,2048]{1,0:T(8,128)}) custom-call(f32[4,8,2,16,1024]{4,3,2,1,0:T(8,128)} %copy-done.4, f32[8,32,2048]{2,1,0:T(8,128)} %copy-done.5, bf16[4,1280,256]{2,1,0:T(8,128)(2,1)} %bitcast.26, ...), custom_call_target="tpu_custom_call" | custom-call | flops 80000000000 | bytes 250000000 | tf_op jit(solution)/shard_map/lead/pallas_call | solution.py:666
  199.8 21.1 %finish.1 = (f32[2,2048,512]{2,1,0:T(8,128)}, f32[256,2048]{1,0:T(8,128)}) custom-call(s32[2]{0:T(128)S(1)} %pad_add_fusion.first_ref, f32[1024,2048]{1,0:T(8,128)} %bitcast.34, bf16[1024,1024]{1,0:T(8,128)(2,1)} %get-tuple-element.18.high_ref, bf16[1024,1024]{1,0:T(8,128)(2,1)} %get-tuple-element.19.low_ref, f32[1024,256]{1,0:T(8,128)S(1)} %bitcast.31, ...), custom_call_target="tpu_custom_call" | custom-call | flops 14000000000 | bytes 25000000 | tf_op jit(solution)/shard_map/finish/pallas_call | solution.py:745
  (3 shorter events, 0.0 us)
Async XLA Ops:
  2.1 0.7 copy-start.2
  2.8 0.9 copy-start.3
  100.0 2.0 copy-start.4
  102.0 1.3 copy-start.5
  103.3 1.5 copy-start
  103.3 1.5 copy-start.1

commit v5 on v4

--- a/solution.py
+++ b/solution.py
@@ -612,9 +612,6 @@
             send_rows(2)
 
     eliminate(inverse_ref, before)
-    for copy in far:
-        copy.wait_recv()
-    send_rows(3)
 
     def turn(i, _):
         here = pl.ds(pl.multiple_of(i * BLOCK, BLOCK), BLOCK)
@@ -622,6 +619,9 @@
         return 0
 
     lax.fori_loop(0, inverse_ref.shape[0] // BLOCK, turn, 0)
+    for copy in far:
+        copy.wait_recv()
+    send_rows(3)
     normal[...] = product(group)
     for copy in exchanges + corners:
         copy.wait()
@@ -741,7 +741,7 @@
 def finish(strip, high, low, rows, normal, first):
     columns = strip.shape[1]
     tile = normal.shape[0]
-    wide = 512
+    wide = 1024
     return pl.pallas_call(
         finish_kernel,
         out_shape=(

time: 224 us -> 225 us (level)
  no operation moved by 1% of the time
where the time goes in v5:
time: 225 us; the launch traced here: 221 us
  Pallas kernels  208 us (92%)
  local copies, waits for them, and re-layouts  5.93 us (3%)
  matrix products  4.57 us (2%)
    pallas_call x1, Pallas kernels, lead(): pl.pallas_call(lead_kernel, out_shape=(jax.ShapeDtypeStruct((width, width...  95 us
    pallas_call x1, Pallas kernels, gather(): pl.pallas_call(gather_kernel, out_shape=(jax.ShapeDtypeStruct((trows, arc...  83.7 us
    pallas_call x1, Pallas kernels, finish(): pl.pallas_call(finish_kernel, out_shape=(jax.ShapeDtypeStruct((PANELS, co...  21.7 us
    pallas_call x1, Pallas kernels, local_basis(): pl.pallas_call(basis_kernel, out_shape=jax.ShapeDtypeStruct((arcs, BLOCK,...  7.67 us
    unnamed x12, local copies, waits for them, and re-layouts  5.83 us

profile of v5, /device:TPU:0, one launch (start us, length us, event | category | flops | bytes accessed | tf_op | source)
XLA Modules:
  0.0 221.5 jit_solution(7912832704920926432)
XLA Ops:
  0.6 0.1 pad_add_fusion.first_ref
  0.7 0.7 broadcast_select_fusion
  1.4 0.7 iota_compare_fusion.2
  2.1 0.0 copy-start.2
  2.1 0.7 copy-done.2
  2.8 0.0 copy-start.3
  2.8 0.9 copy-done.3
  3.7 7.7 %local_basis.1 = bf16[2,128,320]{2,1,0:T(8,128)(2,1)S(1)} custom-call(s32[2]{0:T(128)S(1)} %copy-done.2, bf16[640,128]{1,0:T(8,128)(2,1)S(1)} %copy-done.3), custom_call_target="tpu_custom_call" | custom-call | flops 1000000000 | bytes 30000000 | tf_op jit(solution)/shard_map/local_basis/pallas_call | solution.py:120
  11.4 0.1 fusion.5.regs
  11.5 4.0 %fusion.1 = bf16[1,2,320,2048]{3,2,1,0:T(8,128)(2,1)S(1)} fusion(bf16[1,2,320,2048]{3,2,1,0:T(8,128)(2,1)} %bitcast.32, bf16[2,128,320]{2,1,0:T(8,128)(2,1)S(1)} %local_basis.1, pred[2,320]{1,0:T(4,128)(4,1)S(1)} %iota_compare_fusion.2, bf16[2,320,2048]{2,1,0:T(8,128)(2,1)} %bitcast.33), kind=kOutput, calls=%fused_computation.2 | convolution fusion | flops 676855808 | bytes 8028800 | tf_op jit(solution)/shard_map/alc,talw->tacw/dot_general | solution.py:782
  15.4 0.1 dynamic-slice_bitcast_fusion.1
  15.6 0.1 pad_maximum_fusion.piece
  15.6 0.6 convolution_add_fusion.pivot_part
  16.3 83.7 %gather.1 = (f32[4,8,2,16,1024]{4,3,2,1,0:T(8,128)S(1)}, f32[8,32,2048]{2,1,0:T(8,128)S(1)}, bf16[2,640,2048]{2,1,0:T(8,128)(2,1)}, bf16[4,2,640,256]{3,2,1,0:T(8,128)(2,1)S(1)}) custom-call(bf16[640,2048]{1,0:T(8,128)(2,1)S(1)} %bitcast.29, bf16[2,640,256]{2,1,0:T(8,128)(2,1)S(1)} %pad_maximum_fusion.piece, f32[256,1024]{1,0:T(8,128)S(1)} %convolution_add_fusion.pivot_part, ...), custom_call_target="tpu_custom_call" | custom-call | flops 40000000000 | bytes 250000000 | tf_op jit(solution)/shard_map/gather/pallas_call | solution.py:455
  100.0 0.0 copy-start.4
  100.0 2.0 copy-done.4
  102.0 0.0 copy-start.5
  102.0 1.3 copy-done.5
  103.3 0.0 copy-start
  103.3 0.5 multiply_reduce_fusion
  103.8 0.9 copy-done
  104.8 0.0 copy-done.1
  104.8 95.0 %lead.1 = (bf16[1024,1024]{1,0:T(8,128)(2,1)}, bf16[1024,1024]{1,0:T(8,128)(2,1)}, f32[4,8,32,2048]{3,2,1,0:T(8,128)}, f32[4,8,32,256]{3,2,1,0:T(8,128)S(1)}, f32[256,2048]{1,0:T(8,128)}) custom-call(f32[4,8,2,16,1024]{4,3,2,1,0:T(8,128)} %copy-done.4, f32[8,32,2048]{2,1,0:T(8,128)} %copy-done.5, bf16[4,1280,256]{2,1,0:T(8,128)(2,1)} %bitcast.26, ...), custom_call_target="tpu_custom_call" | custom-call | flops 80000000000 | bytes 250000000 | tf_op jit(solution)/shard_map/lead/pallas_call | solution.py:666
  199.8 21.7 %finish.1 = (f32[2,2048,512]{2,1,0:T(8,128)}, f32[256,2048]{1,0:T(8,128)}) custom-call(s32[2]{0:T(128)S(1)} %pad_add_fusion.first_ref, f32[1024,2048]{1,0:T(8,128)} %bitcast.34, bf16[1024,1024]{1,0:T(8,128)(2,1)} %get-tuple-element.18.high_ref, bf16[1024,1024]{1,0:T(8,128)(2,1)} %get-tuple-element.19.low_ref, f32[1024,256]{1,0:T(8,128)S(1)} %bitcast.31, ...), custom_call_target="tpu_custom_call" | custom-call | flops 14000000000 | bytes 25000000 | tf_op jit(solution)/shard_map/finish/pallas_call | solution.py:745
  (3 shorter events, 0.0 us)
Async XLA Ops:
  2.1 0.7 copy-start.2
  2.8 0.9 copy-start.3
  100.0 2.0 copy-start.4
  102.0 1.3 copy-start.5
  103.3 1.5 copy-start
  103.3 1.5 copy-start.1
